TPU v7x, 512 devices: a whole 4x4x16 slice. The times are simulated.
512 devices in a mesh: gx: 64 (over y, z_hi, x), gy: 8 (over z_lo, core).
Axes of the slice: x: 4, y: 4, z: 16 (z_hi: 4, z_lo: 4; z = z_hi * 4 + z_lo), core: 2. Of those that a mesh axis runs over, the one named last changes fastest.
Arguments:
- field: float32 [20, 256, 256, 256], P(None, 'gx', 'gy'), may hold values from -6 to 6
- spectral_weight: bfloat16 [64, 64, 32, 2, 20, 20], P(None, 'gx', 'gy'), may hold values from -6 to 6
- point_weight: float32 [20, 20], replicated, may hold values from -1.25 to 1.25
- point_bias: float32 [20], replicated, may hold values from -4 to 4
Outputs:
- mixed_field: bfloat16 [20, 256, 256, 256], P(None, 'gx', 'gy')
All inputs are finite; a program needn't handle non-finite values.
Results may differ from a plain program's by a relative error of at most 0.009.
Values may be sent and summed in bfloat16 or wider, within the bound.
No kernel may reach another device: no remote copies, remote signals or barrier semaphores. Data moves between devices by JAX's collectives and lax.ppermute only.
A program may use at most 64 MiB of HBM per device.

v0:
```python
import math

import jax
import jax.numpy as jnp
from jax import lax
from jax.sharding import PartitionSpec as P

NX = 256
NY = 256
NZ = 256
KX = 64
KY = 64
KZ = 32


def kept_freqs(number):
    index = jnp.arange(number, dtype=jnp.int32)
    return jnp.where(index < number // 2, index, index - number)


def phase_angles(first_pos, second_pos, length):
    product = jnp.mod(first_pos[:, None] * second_pos[None, :], length)
    return 2.0 * jnp.pi / length * product.astype(jnp.float32)


def forward_table(length, number):
    theta = phase_angles(jnp.arange(length, dtype=jnp.int32), kept_freqs(number), length)
    scale = 1.0 / math.sqrt(length)
    cosine = jnp.cos(theta) * scale
    sine = jnp.sin(theta) * scale
    return jnp.stack([jnp.stack([cosine, -sine], 1), jnp.stack([sine, cosine], 1)], 0)


def inverse_table(length, number):
    theta = phase_angles(kept_freqs(number), jnp.arange(length, dtype=jnp.int32), length)
    scale = 1.0 / math.sqrt(length)
    cosine = jnp.cos(theta) * scale
    sine = jnp.sin(theta) * scale
    return jnp.stack([jnp.stack([cosine, sine], 1), jnp.stack([-sine, cosine], 1)], 0)


def z_forward_table(length, number):
    theta = phase_angles(
        jnp.arange(length, dtype=jnp.int32), jnp.arange(number, dtype=jnp.int32), length
    )
    scale = 1.0 / math.sqrt(length)
    return jnp.concatenate([jnp.cos(theta), -jnp.sin(theta)], 1) * scale


def z_inverse_table(length, number):
    theta = phase_angles(
        jnp.arange(number, dtype=jnp.int32), jnp.arange(length, dtype=jnp.int32), length
    )
    scale = 1.0 / math.sqrt(length)
    factor = jnp.where(jnp.arange(number) == 0, 1.0, 2.0)[:, None] * scale
    return jnp.stack([factor * jnp.cos(theta), -factor * jnp.sin(theta)], 0)


def mix_modes(modes, weight):
    real_w = weight[:, :, :, 0]
    imag_w = weight[:, :, :, 1]
    real_a = modes[:, :, :, 0]
    imag_a = modes[:, :, :, 1]
    form = "ykzc,kyzco->ykzo"
    real_o = jnp.einsum(form, real_a, real_w, preferred_element_type=jnp.float32) - jnp.einsum(
        form, imag_a, imag_w, preferred_element_type=jnp.float32
    )
    imag_o = jnp.einsum(form, real_a, imag_w, preferred_element_type=jnp.float32) + jnp.einsum(
        form, imag_a, real_w, preferred_element_type=jnp.float32
    )
    return jnp.stack([real_o, imag_o], 3).astype(jnp.bfloat16)


def per_device(field, spectral_weight, point_weight, point_bias):
    channels, x_local, y_local, z_length = field.shape
    x_blocks = lax.axis_size("gx")
    y_blocks = lax.axis_size("gy")
    ky_local = KY // x_blocks
    kz_local = KZ // y_blocks
    column_cells = channels * x_local * y_local
    z_table = z_forward_table(NZ, KZ)
    z_modes = jnp.einsum("zk,cxyz->kcxy", z_table, field, precision=lax.Precision.HIGHEST).astype(
        jnp.bfloat16
    )
    z_modes = z_modes.reshape(2, y_blocks, kz_local, 1, column_cells)
    y_pencil = lax.all_to_all(z_modes, "gy", split_axis=1, concat_axis=3, tiled=True)
    y_pencil = y_pencil.reshape(2, kz_local, y_blocks, channels, x_local, y_local)
    y_table = (
        forward_table(NY, KY)
        .astype(jnp.bfloat16)
        .reshape(2, y_blocks, y_local, 2, x_blocks, ky_local)
    )
    y_modes = jnp.einsum(
        "pzscxy,psyqda->dqazcx", y_pencil, y_table, preferred_element_type=jnp.float32
    ).astype(jnp.bfloat16)
    y_modes = y_modes.reshape(x_blocks, 2 * ky_local, 1, kz_local * channels * x_local)
    x_table = forward_table(NX, KX).astype(jnp.bfloat16)
    x_inverse = inverse_table(NX, KX).astype(jnp.bfloat16)
    x_pencil = lax.all_to_all(y_modes, "gx", split_axis=0, concat_axis=2, tiled=True)
    x_pencil = x_pencil.reshape(2, ky_local, x_blocks, kz_local, channels, x_local)
    x_grouped = x_table.reshape(2, x_blocks, x_local, 2, KX)
    x_modes = jnp.einsum(
        "pasdcx,psxqk->akdqc", x_pencil, x_grouped, preferred_element_type=jnp.float32
    ).astype(jnp.bfloat16)
    spectrum = mix_modes(x_modes, spectral_weight)
    x_split = x_inverse.reshape(2, KX, 2, x_blocks, x_local)
    x_cells = jnp.einsum(
        "akzpc,pkqdx->dqazcx", spectrum, x_split, preferred_element_type=jnp.float32
    ).astype(jnp.bfloat16)
    x_cells = x_cells.reshape(x_blocks, 1, 2 * ky_local, kz_local * channels * x_local)
    y_spectrum = lax.all_to_all(x_cells, "gx", split_axis=0, concat_axis=1, tiled=True)
    y_spectrum = y_spectrum.reshape(x_blocks, 2, ky_local, kz_local, channels, x_local)
    back_form = "spazcx,psaqgy->gqzcxy"
    y_inverse = (
        inverse_table(NY, KY)
        .astype(jnp.bfloat16)
        .reshape(2, x_blocks, ky_local, 2, y_blocks, y_local)
    )
    y_cells = jnp.einsum(
        back_form, y_spectrum, y_inverse, preferred_element_type=jnp.float32
    ).astype(jnp.bfloat16)
    y_cells = y_cells.reshape(y_blocks, 2, 1, kz_local, column_cells)
    z_pencil = lax.all_to_all(y_cells, "gy", split_axis=0, concat_axis=2, tiled=True)
    z_pencil = z_pencil.reshape(2, KZ, column_cells)
    z_inverse = z_inverse_table(NZ, KZ).astype(jnp.bfloat16)
    spectral = jnp.einsum("pkm,pkz->mz", z_pencil, z_inverse, preferred_element_type=jnp.float32)
    spectral = spectral.reshape(channels, x_local, y_local, z_length)
    pointwise = jnp.einsum("cxyz,co->oxyz", field, point_weight, precision=lax.Precision.HIGHEST)
    return jax.nn.gelu(spectral + pointwise + point_bias[:, None, None, None]).astype(jnp.bfloat16)


def solution(mesh):
    in_specs = (P(None, "gx", "gy", None), P(None, "gx", "gy", None, None, None), P(), P())
    out_specs = P(None, "gx", "gy", None)
    return jax.shard_map(
        per_device, mesh=mesh, in_specs=in_specs, out_specs=out_specs, check_vma=False
    )
```

profile of v0, /device:TPU:1, one launch (start us, length us, event | category | flops | bytes accessed | tf_op | source)
XLA Modules:
  0.0 125.6 jit_solution(13739109891067505668)
XLA Ops:
  0.2 1.6 %copy-done = f32[20,4,32,256]{3,2,1,0:T(8,128)S(1)} copy-done((f32[20,4,32,256]{3,2,1,0:T(8,128)S(1)}, f32[20,4,32,256]{3,2,1,0:T(8,128)}, u32[]{:S(2)}) %copy-start) | copy-done | bytes 2621464
  1.7 2.2 %convolution_convert_fusion = bf16[64,20,4,32]{0,3,2,1:T(8,128)(2,1)S(1)} fusion(f32[20,4,32,256]{3,2,1,0:T(8,128)S(1)} %copy-done, f32[256,32]{0,1:T(8,128)S(1)} %get-tuple-element.27, f32[256,32]{0,1:T(8,128)S(1)} %get-tuple-element.28), kind=kOutput, calls=%fused_computation.18 | convolution fusion | flops 503513088 | bytes 3014656 | tf_op jit(solution)/shard_map/zk,cxyz->kcxy/dot_general | solution.py:82
  3.9 2.6 %copy.26 = bf16[64,20,4,32]{3,2,1,0:T(4,128)(2,1)} copy(bf16[64,20,4,32]{0,3,2,1:T(8,128)(2,1)S(1)} %convolution_convert_fusion) | data formatting | bytes 655360 | tf_op jit(solution)/shard_map/convert_element_type | solution.py:82
  6.5 2.9 %reshape.599 = bf16[2,8,4,1,2560]{4,2,1,0,3:T(4,128)(2,1)S(1)} reshape(bf16[64,20,4,32]{3,2,1,0:T(4,128)(2,1)} %copy.26) | data formatting | bytes 655360 | tf_op jit(solution)/shard_map/reshape | solution.py:85
  9.4 0.8 copy.27
  10.3 10.2 %all-to-all-start = ((bf16[2,8,4,1,2560]{4,2,0,3,1:T(4,128)(2,1)}), bf16[2,8,4,1,2560]{4,2,0,3,1:T(4,128)(2,1)S(1)}, u32[]{:S(2)}, u32[]{:S(2)}) async-start(bf16[2,8,4,1,2560]{4,2,0,3,1:T(4,128)(2,1)} %copy.27), calls=%async_computation | async-start | bytes 655360 | tf_op jit(solution)/shard_map/all_to_all | solution.py:86
  20.5 1.3 %negate_convert_fusion.1 = (bf16[1,64,4,1,64]{4,1,2,0,3:T(8,128)(2,1)}, bf16[1,64,4,1,64]{4,1,2,0,3:T(8,128)(2,1)}, bf16[1,64,4,1,64]{4,1,2,0,3:T(8,128)(2,1)}) fusion(s32[64]{0:T(128)S(1)} %compare_select_fusion, s32[64,4]{0,1:T(4,128)S(1)} %multiply_add_fusion.1), kind=kLoop, calls=%fused_computation.103 | loop fusion | flops 327680 | bytes 99584 | tf_op jit(solution)/shard_map/convert.17
  21.8 1.3 %fusion.73 = (bf16[1,64,1,64,4]{3,1,0,4,2:T(8,128)(2,1)}, bf16[1,64,1,64,4]{3,1,0,4,2:T(8,128)(2,1)}, bf16[1,64,1,64,4]{3,1,0,4,2:T(8,128)(2,1)}) fusion(s32[64,4]{0,1:T(4,128)S(1)} %multiply_add_fusion.1, s32[64]{0:T(128)S(1)} %compare_select_fusion), kind=kLoop, calls=%fused_computation.113 | loop fusion | flops 327680 | bytes 99584 | tf_op jit(solution)/shard_map/convert.23
  23.0 0.6 negate_convert_fusion
  23.7 6.9 %all-to-all-done = bf16[2,8,4,1,2560]{4,2,0,3,1:T(4,128)(2,1)S(1)} async-done(((bf16[2,8,4,1,2560]{4,2,0,3,1:T(4,128)(2,1)}), bf16[2,8,4,1,2560]{4,2,0,3,1:T(4,128)(2,1)S(1)}, u32[]{:S(2)}, u32[]{:S(2)}) %all-to-all-start) | async-done | bytes 327712 | tf_op jit(solution)/shard_map/all_to_all | solution.py:86
  30.5 1.8 %reshape.635 = bf16[2,4,8,20,4,32]{5,4,3,1,0,2:T(4,128)(2,1)} reshape(bf16[2,1,4,8,1,2560]{5,2,0,3,4,1:T(4,128)(2,1)S(1)} %bitcast.143) | data formatting | bytes 655360 | tf_op jit(solution)/shard_map/reshape | solution.py:87
  32.3 1.9 %fusion.24 = bf16[64,2,1,4,20,4]{0,4,5,3,1,2:T(8,128)(2,1)S(1)} fusion(bf16[2,4,8,20,4,32]{5,4,3,1,0,2:T(4,128)(2,1)} %reshape.635, bf16[1,8,32,1,64]{4,2,1,0,3:T(8,128)(2,1)S(1)} %get-tuple-element.17, bf16[1,8,32,1,64]{4,2,1,0,3:T(8,128)(2,1)S(1)} %get-tuple-element.16, bf16[1,8,32,1,64]{4,2,1,0,3:T(8,128)(2,1)S(1)} %get-tuple-element.15), kind=kOutput, calls=%fused_computation.25 | convolution fusion | flops 42508288 | bytes 507904 | tf_op jit(solution)/shard_map/pzscxy,psyqda->dqazcx/dot_general | solution.py:93
  34.3 0.8 copy.31
  35.1 15.7 %all-to-all-start.1 = ((bf16[64,2,1,320]{3,1,2,0:T(2,128)(2,1)}), bf16[64,2,1,320]{3,1,2,0:T(2,128)(2,1)S(1)}, u32[]{:S(2)}, u32[]{:S(2)}) async-start(bf16[64,2,1,320]{3,1,2,0:T(2,128)(2,1)} %copy.31), calls=%async_computation.1 | async-start | bytes 196608 | tf_op jit(solution)/shard_map/all_to_all | solution.py:99
  50.8 3.7 %fusion.114 = (bf16[64,1,4,1,20,20]{0,3,5,4,2,1:T(2,128)(2,1)S(1)}, bf16[64,1,4,1,20,20]{0,3,5,4,2,1:T(2,128)(2,1)}) fusion(bf16[64,1,4,2,20,20]{0,3,5,4,2,1:T(2,128)(2,1)} %param.5), kind=kLoop, calls=%fused_computation.174 | loop fusion | bytes 819200 | tf_op jit(solution)/shard_map/slice | solution.py:60
  54.5 12.5 %all-to-all-done.1 = bf16[64,2,1,320]{3,1,2,0:T(2,128)(2,1)S(1)} async-done(((bf16[64,2,1,320]{3,1,2,0:T(2,128)(2,1)}), bf16[64,2,1,320]{3,1,2,0:T(2,128)(2,1)S(1)}, u32[]{:S(2)}, u32[]{:S(2)}) %all-to-all-start.1) | async-done | bytes 81952 | tf_op jit(solution)/shard_map/all_to_all | solution.py:99
  67.0 0.7 copy.142
  67.7 1.7 %copy.33 = bf16[1,2,64,1,320]{2,4,1,3,0:T(8,128)(2,1)} copy(bf16[1,2,64,1,320]{4,2,3,1,0:T(8,128)(2,1)} %bitcast.147) | data formatting | bytes 163840 | tf_op jit(solution)/shard_map/all_to_all | solution.py:99
  69.4 1.3 %fusion.28 = bf16[1,64,4,2,20]{1,4,2,3,0:T(8,128)(2,1)S(1)} fusion(bf16[1,64,4,1,64]{4,1,2,0,3:T(8,128)(2,1)} %get-tuple-element.23, bf16[1,64,4,1,64]{4,1,2,0,3:T(8,128)(2,1)} %get-tuple-element.22, bf16[1,64,4,1,64]{4,1,2,0,3:T(8,128)(2,1)} %get-tuple-element.21, bf16[2,64,4,20,4]{1,4,3,2,0:T(4,128)(2,1)} %bitcast.148), kind=kOutput, calls=%fused_computation.28 | convolution fusion | flops 11020288 | bytes 200704 | tf_op jit(solution)/shard_map/pasdcx,psxqk->akdqc/dot_general | solution.py:102
  70.8 2.3 %fusion.31 = (f32[64,4,20]{0,1,2:T(4,128)S(1)}, f32[64,4,20]{0,1,2:T(4,128)S(1)}, f32[64,4,20]{0,1,2:T(4,128)S(1)}, f32[64,4,20]{0,1,2:T(4,128)S(1)}) fusion(f32[64,4,20]{0,1,2:T(4,128)S(1)} %copy.97, bf16[64,1,4,1,20,20]{0,3,5,4,2,1:T(2,128)(2,1)} %get-tuple-element.12, f32[64,4,20]{0,1,2:T(4,128)S(1)} %copy.96, ...), kind=kLoop, calls=%fused_computation.35 | loop fusion | flops 1003520 | bytes 532480
  73.5 0.8 copy.38
  74.3 4.6 %all-to-all-start.2 = ((bf16[64,1,2,320]{3,2,1,0:T(2,128)(2,1)}), bf16[64,1,2,320]{3,2,1,0:T(2,128)(2,1)S(1)}, u32[]{:S(2)}, u32[]{:S(2)}) async-start(bf16[64,1,2,320]{3,2,1,0:T(2,128)(2,1)} %copy.38), calls=%async_computation.2 | async-start | bytes 196608 | tf_op jit(solution)/shard_map/all_to_all | solution.py:111
  78.9 0.6 fusion.72
  79.5 15.4 %all-to-all-done.2 = bf16[64,1,2,320]{3,2,1,0:T(2,128)(2,1)S(1)} async-done(((bf16[64,1,2,320]{3,2,1,0:T(2,128)(2,1)}), bf16[64,1,2,320]{3,2,1,0:T(2,128)(2,1)S(1)}, u32[]{:S(2)}, u32[]{:S(2)}) %all-to-all-start.2) | async-done | bytes 81952 | tf_op jit(solution)/shard_map/all_to_all | solution.py:111
  95.1 0.6 fusion.14
  95.7 1.7 %copy.91 = bf16[8,2,4,20,4,32]{5,4,3,2,1,0:T(4,128)(2,1)} copy(bf16[8,2,4,20,4,32]{5,3,4,2,0,1:T(8,128)(2,1)S(1)} %fusion.14) | data formatting | bytes 655360 | tf_op jit(solution)/shard_map/reshape | solution.py:122
  97.4 3.5 %reshape.636 = bf16[8,2,1,4,2560]{4,3,1,2,0:T(4,128)(2,1)} reshape(bf16[8,2,4,20,4,32]{5,4,3,2,1,0:T(4,128)(2,1)} %copy.91) | data formatting | bytes 655360 | tf_op jit(solution)/shard_map/reshape | solution.py:122
  100.9 7.1 %all-to-all-start.3 = ((bf16[8,2,1,4,2560]{4,3,1,2,0:T(4,128)(2,1)}), bf16[8,2,1,4,2560]{4,3,1,2,0:T(4,128)(2,1)S(1)}, u32[]{:S(2)}, u32[]{:S(2)}) async-start(bf16[8,2,1,4,2560]{4,3,1,2,0:T(4,128)(2,1)} %reshape.636), calls=%async_computation.3 | async-start | bytes 655360 | tf_op jit(solution)/shard_map/all_to_all | solution.py:123
  108.3 5.6 %fusion = f32[20,4,32,256]{3,0,2,1:T(8,128)} fusion(f32[20,4,32,256]{3,2,1,0:T(8,128)S(1)} %copy-done, f32[20,20]{1,0:T(8,128)S(1)} %copy-done.4), kind=kOutput, calls=%fused_computation.2 | convolution fusion | flops 157286400 | bytes 5244480 | tf_op jit(solution)/shard_map/cxyz,co->oxyz/dot_general | solution.py:128
  113.8 4.3 %all-to-all-done.3 = bf16[8,2,1,4,2560]{4,3,1,2,0:T(4,128)(2,1)S(1)} async-done(((bf16[8,2,1,4,2560]{4,3,1,2,0:T(4,128)(2,1)}), bf16[8,2,1,4,2560]{4,3,1,2,0:T(4,128)(2,1)S(1)}, u32[]{:S(2)}, u32[]{:S(2)}) %all-to-all-start.3) | async-done | bytes 327712 | tf_op jit(solution)/shard_map/all_to_all | solution.py:123
  118.4 1.8 %reshape.637 = bf16[20,4,32,32,2]{2,1,0,4,3:T(4,128)(2,1)} reshape(bf16[2560,32,2]{0,2,1:T(2,128)(2,1)S(1)} %bitcast.144) | data formatting | bytes 655360 | tf_op jit(solution)/shard_map/pkm,pkz->mz/dot_general | solution.py:126
  120.1 5.5 %fusion.9 = bf16[20,4,32,256]{3,2,1,0:T(8,128)(2,1)} fusion(f32[20,4,32,256]{3,0,2,1:T(8,128)} %fusion, bf16[20,4,32,32,2]{2,1,0,4,3:T(4,128)(2,1)} %reshape.637, f32[20]{0:T(128)S(1)} %copy-done.5, bf16[1,32,256]{2,1,0:T(8,128)(2,1)S(1)} %get-tuple-element.29, bf16[1,32,256]{2,1,0:T(8,128)(2,1)S(1)} %get-tuple-element.30), kind=kOutput, calls=%fused_computation.11 | convolution fusion | flops 91111424 | bytes 4292688 | tf_op jit(solution)/shard_map/pkm,pkz->mz/dot_general | solution.py:126
  (28 shorter events, 1.3 us)
Async XLA Ops:
  0.0 1.7 %copy-start = (f32[20,4,32,256]{3,2,1,0:T(8,128)S(1)}, f32[20,4,32,256]{3,2,1,0:T(8,128)}, u32[]{:S(2)}) copy-start(f32[20,4,32,256]{3,2,1,0:T(8,128)} %param.4) | copy-start | bytes 7864324
  10.3 20.3 %all-to-all-start = ((bf16[2,8,4,1,2560]{4,2,0,3,1:T(4,128)(2,1)}), bf16[2,8,4,1,2560]{4,2,0,3,1:T(4,128)(2,1)S(1)}, u32[]{:S(2)}, u32[]{:S(2)}) async-start(bf16[2,8,4,1,2560]{4,2,0,3,1:T(4,128)(2,1)} %copy.27), calls=%async_computation | async-start | bytes 655360 | tf_op jit(solution)/shard_map/all_to_all | solution.py:86
  35.1 32.0 %all-to-all-start.1 = ((bf16[64,2,1,320]{3,1,2,0:T(2,128)(2,1)}), bf16[64,2,1,320]{3,1,2,0:T(2,128)(2,1)S(1)}, u32[]{:S(2)}, u32[]{:S(2)}) async-start(bf16[64,2,1,320]{3,1,2,0:T(2,128)(2,1)} %copy.31), calls=%async_computation.1 | async-start | bytes 196608 | tf_op jit(solution)/shard_map/all_to_all | solution.py:99
  67.7 5.4 %copy-start.1 = (bf16[1,64,1,64,4]{3,1,0,4,2:T(8,128)(2,1)S(1)}, bf16[1,64,1,64,4]{3,1,0,4,2:T(8,128)(2,1)}, u32[]{:S(2)}) copy-start(bf16[1,64,1,64,4]{3,1,0,4,2:T(8,128)(2,1)} %get-tuple-element.24) | copy-start | bytes 98308
  69.4 3.7 %copy-start.2 = (bf16[1,64,1,64,4]{3,1,0,4,2:T(8,128)(2,1)S(1)}, bf16[1,64,1,64,4]{3,1,0,4,2:T(8,128)(2,1)}, u32[]{:S(2)}) copy-start(bf16[1,64,1,64,4]{3,1,0,4,2:T(8,128)(2,1)} %get-tuple-element.25) | copy-start | bytes 98308
  69.4 3.7 %copy-start.3 = (bf16[1,64,1,64,4]{3,1,0,4,2:T(8,128)(2,1)S(1)}, bf16[1,64,1,64,4]{3,1,0,4,2:T(8,128)(2,1)}, u32[]{:S(2)}) copy-start(bf16[1,64,1,64,4]{3,1,0,4,2:T(8,128)(2,1)} %get-tuple-element.26) | copy-start | bytes 98308
  74.3 20.7 %all-to-all-start.2 = ((bf16[64,1,2,320]{3,2,1,0:T(2,128)(2,1)}), bf16[64,1,2,320]{3,2,1,0:T(2,128)(2,1)S(1)}, u32[]{:S(2)}, u32[]{:S(2)}) async-start(bf16[64,1,2,320]{3,2,1,0:T(2,128)(2,1)} %copy.38), calls=%async_computation.2 | async-start | bytes 196608 | tf_op jit(solution)/shard_map/all_to_all | solution.py:111
  95.7 12.5 %copy-start.4 = (f32[20,20]{1,0:T(8,128)S(1)}, f32[20,20]{1,0:T(8,128)}, u32[]{:S(2)}) copy-start(f32[20,20]{1,0:T(8,128)} %param.6) | copy-start | bytes 4804
  100.9 17.2 %all-to-all-start.3 = ((bf16[8,2,1,4,2560]{4,3,1,2,0:T(4,128)(2,1)}), bf16[8,2,1,4,2560]{4,3,1,2,0:T(4,128)(2,1)S(1)}, u32[]{:S(2)}, u32[]{:S(2)}) async-start(bf16[8,2,1,4,2560]{4,3,1,2,0:T(4,128)(2,1)} %reshape.636), calls=%async_computation.3 | async-start | bytes 655360 | tf_op jit(solution)/shard_map/all_to_all | solution.py:123
  108.3 11.9 %copy-start.5 = (f32[20]{0:T(128)S(1)}, f32[20]{0:T(128)}, u32[]{:S(2)}) copy-start(f32[20]{0:T(128)} %param.7) | copy-start | bytes 244
where the time goes:
time: 126 us
  waiting for transfers between devices  39.1 us (31%)
  starting transfers between devices  37.7 us (30%)
  local copies, waits for them, and re-layouts  24.9 us (20%)
  matrix products  17.3 us (14%)
  other arithmetic  6.41 us (5%)
    all_to_all x1, starting transfers between devices, per_device(): lax.all_to_all(y_modes, 'gx', split_axis=0, concat_axis=2, tiled=True)  15.7 us
    all_to_all x1, waiting for transfers between devices, per_device(): lax.all_to_all(x_cells, 'gx', split_axis=0, concat_axis=1, tiled=True)  15.4 us
    all_to_all x1, waiting for transfers between devices, per_device(): lax.all_to_all(y_modes, 'gx', split_axis=0, concat_axis=2, tiled=True)  12.5 us
    all_to_all x1, starting transfers between devices, per_device(): lax.all_to_all(z_modes, 'gy', split_axis=1, concat_axis=3, tiled=True)  10.2 us
    all_to_all x1, starting transfers between devices, per_device(): lax.all_to_all(y_cells, 'gy', split_axis=0, concat_axis=2, tiled=True)  7.14 us
    all_to_all x1, waiting for transfers between devices, per_device(): lax.all_to_all(z_modes, 'gy', split_axis=1, concat_axis=3, tiled=True)  6.85 us
    dot_general x1, matrix products, per_device(): jnp.einsum('cxyz,co->oxyz', field, point_weight, precision=lax.Precision....  5.57 us
    dot_general x1, matrix products, per_device(): jnp.einsum('pkm,pkz->mz', z_pencil, z_inverse, preferred_element_type=jnp...  5.48 us
  transfers between devices with their start and end apart: 4, of which 4 were waited for; matrix products, arithmetic and copies ran while one was open for 11% of the time, Pallas kernels for 0%

commit v1 on v0

v1 whole, which is shorter than its diff:
```python
import functools
import math

import jax
import jax.numpy as jnp
import numpy as np
from jax import lax
from jax.experimental import pallas as pl
from jax.experimental.pallas import tpu as pltpu
from jax.sharding import PartitionSpec as P

C = 20
NX = 256
NY = 256
NZ = 256
KX = 64
KY = 64
KZ = 32
F32 = jnp.float32
BF16 = jnp.bfloat16
MIB = 1 << 20
CHUNK = 4
LANES = 128


def kept_freqs(number):
    index = np.arange(number)
    return np.where(index < number // 2, index, index - number)


def waves(first_pos, second_pos, length):
    theta = 2.0 * np.pi / length * np.mod(np.multiply.outer(first_pos, second_pos), length)
    return np.cos(theta), np.sin(theta)


def z_table(gy, forward):
    shape = (2 * KZ, NZ)
    row = lax.broadcasted_iota(jnp.int32, shape, 0)
    cell = lax.broadcasted_iota(jnp.int32, shape, 1)
    own = KZ // gy
    mode = row // (2 * own) * own + row % own
    imaginary = row // own % 2 == 1
    turn = jnp.where(imaginary, NZ // 4, 0)
    angle = ((mode * cell + turn) % NZ).astype(F32) * (2.0 * math.pi / NZ)
    scale = 1.0 / math.sqrt(NZ)
    if not forward:
        scale = jnp.where(mode == 0, scale, 2.0 * scale)
    return (jnp.cos(angle) * scale).astype(BF16)


def y_waves(gy, xl, order):
    both = np.stack(waves(kept_freqs(KY), np.arange(NY), NY))[order] / math.sqrt(NY)
    both = both.reshape(2, KY, gy, NY // gy)
    table = np.einsum("tksy,ab->tsakby", both, np.eye(xl))
    return table.reshape(2, gy, xl * KY, xl * (NY // gy)).astype(jnp.bfloat16)


def x_pair(gx, xl, forward):
    cosine, sine = waves(kept_freqs(KX), np.arange(NX), NX)
    sign = 1.0 if forward else -1.0
    pair = np.stack([np.stack([cosine, -sign * sine]), np.stack([sign * sine, cosine])])
    if not forward:
        pair = pair.swapaxes(0, 1)
    pair = pair.reshape(2, 2, KX, gx, xl) / math.sqrt(NX)
    return pair.transpose(4, 3, 0, 1, 2).reshape(xl, 2 * gx, 2 * KX).astype(jnp.bfloat16)


def dot(a, b, ca, cb):
    return lax.dot_general(a, b, (((ca,), (cb,)), ((), ())), preferred_element_type=F32)


def vmem():
    return pl.BlockSpec(memory_space=pltpu.VMEM)


def hbm():
    return pl.BlockSpec(memory_space=pltpu.HBM)


def wide(ref, *index):
    *outer, last = index
    return jnp.concatenate([ref[(*outer, last)], ref[(*outer, last + 1)]], axis=1)


def rotated(gx, gy):
    step = gx // gy
    return [[(j + step * g) % gx * gy + g for j in range(gx)] for g in range(gy)]


def turn(cells, gx, gy, back):
    shift = 2 * (gx // gy) * lax.axis_index("gy")
    if not back:
        shift = lax.rem(2 * gx - shift, 2 * gx)
    return pltpu.roll(cells, shift, 0)


def z_forward_kernel(field_ref, _, out_ref, rows):
    channels, xl, yl, nz = field_ref.shape
    table = z_table(out_ref.shape[0], True)
    for c in range(channels):
        cells = field_ref[c].reshape(xl * yl, nz).astype(BF16)
        rows[pl.ds(c, 2 * KZ, stride=channels), :] = dot(table, cells, 1, 1)
    out_ref[...] = rows[...].astype(BF16).reshape(out_ref.shape)


def y_forward_kernel(modes_ref, table_ref, out_ref, rows):
    gy, size, _ = modes_ref.shape
    columns = size // 2
    straight, crossed = 0.0, 0.0
    for s in range(0, gy, 2):
        block = wide(modes_ref, s)
        straight += dot(wide(table_ref, 0, s), block, 1, 1)
        crossed += dot(wide(table_ref, 1, s), block, 1, 1)
    real = straight[:, :columns] + crossed[:, columns:]
    imag = straight[:, columns:] - crossed[:, :columns]
    for q, part in enumerate((real, imag)):
        pieces = [part[i : i + KY] for i in range(0, part.shape[0], KY)]
        spare = rows.shape[0] * LANES - out_ref.shape[2]
        pieces = jnp.concatenate([*pieces, jnp.zeros((KY, spare), F32)], axis=1)
        for i in range(rows.shape[0]):
            rows[i, pl.ds(q, KY, stride=2), :] = pieces[:, i * LANES : (i + 1) * LANES]
    joined = jnp.concatenate([rows[i] for i in range(rows.shape[0])], axis=1)
    joined = turn(joined, out_ref.shape[0], gy, False)
    out_ref[...] = joined[:, : out_ref.shape[2]].reshape(out_ref.shape).astype(BF16)


def mix_kernel(gy, modes_ref, forward_ref, weight_ref, inverse_ref, out_ref):
    xl = forward_ref.shape[0]
    columns = modes_ref.shape[2] // xl
    kz = columns // C
    gx = modes_ref.shape[0]
    cells = modes_ref[...].astype(F32).reshape(-1, modes_ref.shape[2])
    spare = jnp.zeros((2 * gx, -cells.shape[1] % LANES), F32)
    cells = turn(jnp.concatenate([cells, spare], axis=1), gx, gy, True)
    modes = jnp.zeros((columns, 2 * KX), F32)
    for x in range(xl):
        block = cells[:, x * columns : (x + 1) * columns].astype(BF16)
        modes += dot(block, forward_ref[x], 0, 0)
    turned = pltpu.roll(modes, KX, 1)
    low = lax.broadcasted_iota(jnp.int32, (C, 2 * KX), 1) < KX
    spectrum = []
    for k in range(kz):
        straight = jnp.zeros((C, 2 * KX), F32)
        crossed = jnp.zeros((C, 2 * KX), F32)
        for c in range(C):
            row = k * C + c
            weight = weight_ref[row].astype(F32)
            straight += weight * modes[row : row + 1]
            crossed += weight * turned[row : row + 1]
        real = straight - pltpu.roll(straight, KX, 1)
        imag = crossed + pltpu.roll(crossed, KX, 1)
        spectrum.append(jnp.where(low, real, imag))
    spectrum = jnp.concatenate(spectrum, axis=0).astype(BF16)
    back = [dot(inverse_ref[x], spectrum, 1, 1) for x in range(xl)]
    back = turn(jnp.concatenate([*back, spare], axis=1), gx, gy, False)
    out_ref[...] = back[:, : out_ref.shape[2]].reshape(out_ref.shape).astype(BF16)


def y_inverse_kernel(modes_ref, table_ref, out_ref, rows):
    gy, size, lanes = out_ref.shape
    columns = size // 2
    slots = range(rows.shape[0])
    whole = modes_ref[...].astype(F32).reshape(rows.shape[1], -1)
    spare = jnp.zeros((rows.shape[1], rows.shape[0] * LANES - whole.shape[1]), F32)
    padded = turn(jnp.concatenate([whole, spare], axis=1), modes_ref.shape[0], gy, True)
    for i in slots:
        rows[i] = padded[:, i * LANES : (i + 1) * LANES]
    real = jnp.concatenate([rows[i, pl.ds(0, KY, stride=2), :] for i in slots], axis=1)
    imag = jnp.concatenate([rows[i, pl.ds(1, KY, stride=2), :] for i in slots], axis=1)
    cells = []
    for i in range(0, whole.shape[1], columns):
        cells.append(jnp.concatenate([real[:, i : i + columns], imag[:, i : i + columns]], axis=1))
    cells = jnp.concatenate(cells, axis=0).astype(BF16)
    for s in range(0, gy, 2):
        straight = dot(cells, wide(table_ref, 1, s), 0, 0)
        crossed = dot(cells, wide(table_ref, 0, s), 0, 0)
        real = (straight[:columns] - crossed[columns:]).astype(BF16)
        imag = (crossed[:columns] + straight[columns:]).astype(BF16)
        for h in range(2):
            out_ref[s + h, :columns] = real[:, h * lanes : (h + 1) * lanes]
            out_ref[s + h, columns:] = imag[:, h * lanes : (h + 1) * lanes]


def output_kernel(
    modes_ref, field_ref, point_ref, bias_ref, out_ref, rows, point, result, sems
):
    channels, xl, yl, nz = field_ref.shape
    sub = 8
    size = channels * sub
    row = lax.broadcasted_iota(jnp.int32, (size, channels), 0) // sub
    col = lax.broadcasted_iota(jnp.int32, (size, channels), 1)
    pick = jnp.where(row == col, 1.0, 0.0).astype(BF16)
    tall = dot(pick, point_ref[...].astype(BF16), 1, 1).astype(BF16)
    first = lax.broadcasted_iota(jnp.int32, (size, size), 0) % sub
    second = lax.broadcasted_iota(jnp.int32, (size, size), 1) % sub
    spread = jnp.where(first == second, dot(tall, pick, 1, 1), 0.0).astype(BF16)
    for x in range(xl):
        for y in range(0, yl, sub):
            cells = field_ref[:, x, y : y + sub, :].reshape(size, nz).astype(BF16)
            point[:, x, y : y + sub, :] = dot(spread, cells, 1, 0).reshape(channels, sub, nz)
    rows[...] = modes_ref[...].reshape(rows.shape).astype(F32)
    table = z_table(modes_ref.shape[0], False)
    copies = []
    for c in range(channels):
        modes = rows[pl.ds(c, 2 * KZ, stride=channels), :].astype(BF16)
        value = point[c].reshape(xl * yl, nz) + dot(modes, table, 0, 0) + bias_ref[c]
        inner = value * (0.7978845608028654 + 0.035677408136300125 * value * value)
        half = 0.5 * value
        result[c] = (half + half * jnp.tanh(inner)).astype(BF16).reshape(xl, yl, nz)
        if c % CHUNK == CHUNK - 1:
            part = pl.ds(c + 1 - CHUNK, CHUNK)
            copies.append(
                pltpu.make_async_copy(result.at[part], out_ref.at[part], sems.at[c // CHUNK])
            )
            copies[-1].start()
    for copy in copies:
        copy.wait()


def per_device(field, spectral_weight, point_weight, point_bias):
    gx = lax.axis_size("gx")
    gy = lax.axis_size("gy")
    channels, xl, yl, nz = field.shape
    columns = KZ // gy * channels
    lanes = xl * yl
    pencil = jax.ShapeDtypeStruct((gy, 2 * columns, lanes), BF16)
    mode_rows = jax.ShapeDtypeStruct((gx, 2, xl * columns), BF16)
    small = pltpu.CompilerParams(vmem_limit_bytes=16 * MIB)

    def exchange(blocks):
        groups = rotated(gx, gy)
        return lax.all_to_all(blocks, ("gx", "gy"), 0, 0, axis_index_groups=groups, tiled=True)

    weight = spectral_weight[:, 0].transpose(1, 3, 4, 2, 0).reshape(columns, channels, 2 * KX)
    modes = pl.pallas_call(
        z_forward_kernel,
        in_specs=[vmem(), pl.BlockSpec(memory_space=pl.ANY)],
        out_specs=vmem(),
        out_shape=pencil,
        scratch_shapes=[pltpu.VMEM((2 * KZ * channels, lanes), F32)],
        compiler_params=small,
        name="z_forward",
    )(field, weight)

    modes = lax.all_to_all(modes, "gy", 0, 0, tiled=True)
    modes = pl.pallas_call(
        y_forward_kernel,
        in_specs=[vmem(), vmem()],
        out_specs=vmem(),
        out_shape=mode_rows,
        scratch_shapes=[pltpu.VMEM((pl.cdiv(xl * columns, LANES), 2 * gx, LANES), F32)],
        compiler_params=small,
        name="y_forward",
    )(modes, y_waves(gy, xl, [0, 1]))

    modes = exchange(modes)

    modes = pl.pallas_call(
        functools.partial(mix_kernel, gy),
        in_specs=[vmem(), vmem(), vmem(), vmem()],
        out_specs=vmem(),
        out_shape=mode_rows,
        compiler_params=small,
        name="mix",
    )(modes, x_pair(gx, xl, True), weight, x_pair(gx, xl, False))

    modes = exchange(modes)

    modes = pl.pallas_call(
        y_inverse_kernel,
        in_specs=[vmem(), vmem()],
        out_specs=vmem(),
        out_shape=pencil,
        scratch_shapes=[pltpu.VMEM((pl.cdiv(xl * columns, LANES), 2 * gx, LANES), F32)],
        compiler_params=small,
        name="y_inverse",
    )(modes, y_waves(gy, xl, [1, 0]))

    modes = lax.all_to_all(modes, "gy", 0, 0, tiled=True)

    return pl.pallas_call(
        output_kernel,
        in_specs=[vmem(), vmem(), vmem(), pl.BlockSpec(memory_space=pltpu.SMEM)],
        out_specs=hbm(),
        out_shape=jax.ShapeDtypeStruct(field.shape, BF16),
        scratch_shapes=[
            pltpu.VMEM((2 * KZ * channels, lanes), F32),
            pltpu.VMEM(field.shape, F32),
            pltpu.VMEM(field.shape, BF16),
            pltpu.SemaphoreType.DMA((channels // CHUNK,)),
        ],
        compiler_params=small,
        name="output",
    )(modes, field, point_weight, point_bias)


def solution(mesh):
    in_specs = (P(None, "gx", "gy", None), P(None, "gx", "gy", None, None, None), P(), P())
    out_specs = P(None, "gx", "gy", None)
    return jax.shard_map(
        per_device, mesh=mesh, in_specs=in_specs, out_specs=out_specs, check_vma=False
    )
```

time: 126 us -> 99.1 us (0.79)
  blocking collectives: 0 us -> 88.3 us
  waiting for transfers between devices: 39.1 us -> 0 us
  starting transfers between devices: 37.7 us -> 0 us
  local copies, waits for them, and re-layouts: 24.9 us -> 4.04 us
  matrix products: 17.3 us -> 0 us
  other arithmetic: 6.41 us -> 0 us
  Pallas kernels: 0 us -> 6.37 us
    all_to_all x0 -> x4, blocking collectives: none -> 88.3 us  [the longest x2 46.5 us: exchange(): lax.all_to_all(blocks, ('gx', 'gy'), 0, 0, axis_index_groups=groups, tile...]
    all_to_all x4 -> x0, waiting for transfers between devices: 39.1 us -> none  [the longest x1 15.4 us: per_device(): lax.all_to_all(x_cells, 'gx', split_axis=0, concat_axis=1, tiled=True)]
    all_to_all x4 -> x0, starting transfers between devices: 37.7 us -> none  [the longest x1 15.7 us: per_device(): lax.all_to_all(y_modes, 'gx', split_axis=0, concat_axis=2, tiled=True)]
    dot_general x7 -> x0, matrix products: 17.3 us -> none  [the longest x1 5.57 us: per_device(): jnp.einsum('cxyz,co->oxyz', field, point_weight, precision=lax.Precision....]
    reshape x7 -> x1, local copies, waits for them, and re-layouts: 12.3 us -> 2.28 us  [per_device(): spectral_weight[:, 0].transpose(1, 3, 4, 2, 0)]
    pallas_call x0 -> x5, Pallas kernels: none -> 6.37 us  [the longest x1 3.2 us: per_device(): pl.pallas_call(output_kernel, in_specs=[vmem(), vmem(), vmem(), pl.BlockS...]
    another operation x7 -> x0, other arithmetic: 3.95 us -> none
    slice x1 -> x0, local copies, waits for them, and re-layouts: 3.73 us -> none  [mix_modes(): real_w = weight[:, :, :, 0]]
  transfers between devices with their start and end apart: 4 -> 0, of which waited for: 4 -> 0; matrix products, arithmetic and copies ran while one was open for 11% -> 0% of each run, Pallas kernels for 0% -> 0%
where the time goes in v1:
time: 99.1 us; the launch traced here: 98.8 us
  blocking collectives  88.3 us (89%)
  Pallas kernels  6.37 us (6%)
  local copies, waits for them, and re-layouts  4.04 us (4%)
    all_to_all x2, blocking collectives, exchange(): lax.all_to_all(blocks, ('gx', 'gy'), 0, 0, axis_index_groups=groups, tile...  46.5 us
    all_to_all x2, blocking collectives, per_device(): modes = lax.all_to_all(modes, 'gy', 0, 0, tiled=True)  41.8 us
    pallas_call x1, Pallas kernels, per_device(): pl.pallas_call(output_kernel, in_specs=[vmem(), vmem(), vmem(), pl.BlockS...  3.2 us
    reshape x1, local copies, waits for them, and re-layouts, per_device(): spectral_weight[:, 0].transpose(1, 3, 4, 2, 0)  2.28 us

profile of v1, /device:TPU:1, one launch (start us, length us, event | category | flops | bytes accessed | tf_op | source)
XLA Modules:
  0.0 98.8 jit_solution(4529817932474641299)
XLA Ops:
  0.0 0.0 copy-start.3
  0.0 2.3 %reshape.4._.weight_ref = bf16[80,20,128]{2,1,0:T(8,128)(2,1)S(1)} reshape(bf16[4,20,20,2,64]{4,3,2,1,0:T(2,128)(2,1)} %bitcast.3) | data formatting | bytes 819200 | tf_op jit(solution)/shard_map/reshape | solution.py:234
  2.3 0.0 copy-start
  2.3 1.7 %copy-done = f32[20,4,32,256]{3,2,1,0:T(8,128)S(1)} copy-done((f32[20,4,32,256]{3,2,1,0:T(8,128)S(1)}, f32[20,4,32,256]{3,2,1,0:T(8,128)}, u32[]{:S(2)}) %copy-start) | copy-done | bytes 2621464
  4.0 0.0 copy-start.4
  4.0 0.0 copy-start.2
  4.0 0.8 z_forward.1
  4.8 19.7 %all_to_all.20.modes_ref = bf16[8,160,128]{2,1,0:T(8,128)(2,1)S(1)} all-to-all(bf16[8,160,128]{2,1,0:T(8,128)(2,1)S(1)} %z_forward.1), channel_id=1, replica_groups=mesh['gx'=64,'gy'=8] {'gy'}, dimensions={0} | all-to-all | bytes 655360 | tf_op jit(solution)/shard_map/all_to_all | solution.py:245
  24.5 0.0 copy-done.3
  24.5 0.0 copy-start.1
  24.5 0.0 copy-start.5
  24.5 0.0 copy-start.6
  24.5 0.8 y_forward.1
  25.3 24.5 %all_to_all.21.modes_ref = bf16[64,2,320]{2,1,0:T(2,128)(2,1)S(1)} all-to-all(bf16[64,2,320]{2,1,0:T(2,128)(2,1)S(1)} %y_forward.1), channel_id=1, replica_groups={{0,8,16,24,32,40,48,56,64,72,80,88,96,104,112,120,128,136,144,152,160,1..., dimensions={0} | all-to-all | bytes 163840 | tf_op jit(solution)/shard_map/all_to_all | solution.py:232
  49.8 0.0 copy-done.4
  49.8 1.0 %mix.1 = bf16[64,2,320]{2,1,0:T(2,128)(2,1)S(1)} custom-call(bf16[64,2,320]{2,1,0:T(2,128)(2,1)S(1)} %all_to_all.21.modes_ref, bf16[4,128,128]{2,1,0:T(8,128)(2,1)S(1)} %copy-done.4, bf16[80,20,128]{2,1,0:T(8,128)(2,1)S(1)} %reshape.4._.weight_ref, bf16[4,128,128]{2,1,0:T(8,128)(2,1)S(1)} %copy-done.4), custom_call_target="tpu_custom_call" | custom-call | tf_op jit(solution)/shard_map/mix/pallas_call | solution.py:258
  50.9 22.0 %all_to_all.22.modes_ref = bf16[64,2,320]{2,1,0:T(2,128)(2,1)S(1)} all-to-all(bf16[64,2,320]{2,1,0:T(2,128)(2,1)S(1)} %mix.1), channel_id=1, replica_groups={{0,8,16,24,32,40,48,56,64,72,80,88,96,104,112,120,128,136,144,152,160,1..., dimensions={0} | all-to-all | bytes 163840 | tf_op jit(solution)/shard_map/all_to_all | solution.py:232
  72.9 0.0 copy-done.2
  72.9 0.5 y_inverse.1
  73.4 22.2 %all_to_all.23.modes_ref = bf16[8,160,128]{2,1,0:T(8,128)(2,1)S(1)} all-to-all(bf16[8,160,128]{2,1,0:T(8,128)(2,1)S(1)} %y_inverse.1), channel_id=1, replica_groups=mesh['gx'=64,'gy'=8] {'gy'}, dimensions={0} | all-to-all | bytes 655360 | tf_op jit(solution)/shard_map/all_to_all | solution.py:279
  95.6 0.0 copy-done.1
  95.6 0.0 copy-done.5
  95.6 0.0 copy-done.6
  95.6 3.2 %output.1 = bf16[20,4,32,256]{3,2,1,0:T(8,128)(2,1)} custom-call(bf16[8,160,128]{2,1,0:T(8,128)(2,1)S(1)} %all_to_all.23.modes_ref, f32[20,4,32,256]{3,2,1,0:T(8,128)S(1)} %copy-done.1, f32[20,20]{1,0:T(8,128)S(1)} %copy-done.5, f32[20]{0:T(128)S(1)} %copy-done.6), custom_call_target="tpu_custom_call" | custom-call | tf_op jit(solution)/shard_map/output/pallas_call | solution.py:281
Async XLA Ops:
  0.0 24.5 %copy-start.3 = (bf16[2,8,256,128]{3,2,1,0:T(8,128)(2,1)S(1)}, bf16[2,8,256,128]{3,2,1,0:T(8,128)(2,1)}, u32[]{:S(2)}) copy-start(bf16[2,8,256,128]{3,2,1,0:T(8,128)(2,1)} %constant.6.clone.table_ref) | copy-start | bytes 3145732
  2.3 1.7 %copy-start = (f32[20,4,32,256]{3,2,1,0:T(8,128)S(1)}, f32[20,4,32,256]{3,2,1,0:T(8,128)}, u32[]{:S(2)}) copy-start(f32[20,4,32,256]{3,2,1,0:T(8,128)} %field_ref.3) | copy-start | bytes 7864324
  4.0 45.8 %copy-start.4 = (bf16[4,128,128]{2,1,0:T(8,128)(2,1)S(1)}, bf16[4,128,128]{2,1,0:T(8,128)(2,1)}, u32[]{:S(2)}) copy-start(bf16[4,128,128]{2,1,0:T(8,128)(2,1)} %constant.7.clone.forward_ref.inverse_ref) | copy-start | bytes 393220
  4.0 68.8 %copy-start.2 = (bf16[2,8,256,128]{3,2,1,0:T(8,128)(2,1)S(1)}, bf16[2,8,256,128]{3,2,1,0:T(8,128)(2,1)}, u32[]{:S(2)}) copy-start(bf16[2,8,256,128]{3,2,1,0:T(8,128)(2,1)} %constant.8.clone.table_ref) | copy-start | bytes 3145732
  24.5 71.1 %copy-start.1 = (f32[20,4,32,256]{3,2,1,0:T(8,128)S(1)}, f32[20,4,32,256]{3,2,1,0:T(8,128)}, u32[]{:S(2)}) copy-start(f32[20,4,32,256]{3,2,1,0:T(8,128)} %field_ref.3) | copy-start | bytes 7864324
  24.5 71.1 %copy-start.5 = (f32[20,20]{1,0:T(8,128)S(1)}, f32[20,20]{1,0:T(8,128)}, u32[]{:S(2)}) copy-start(f32[20,20]{1,0:T(8,128)} %point_ref.1) | copy-start | bytes 4804
  24.5 71.1 %copy-start.6 = (f32[20]{0:T(128)S(1)}, f32[20]{0:T(128)}, u32[]{:S(2)}) copy-start(f32[20]{0:T(128)} %bias_ref.1) | copy-start | bytes 244

commit v2 on v1

--- a/solution.py
+++ b/solution.py
@@ -33,12 +33,21 @@
     return np.cos(theta), np.sin(theta)
 
 
+def near_order(j, gy):
+    return (j // 2) ^ ((gy - 2) * (j % 2)) if gy > 2 else j
+
+
+def far_order(j, gx):
+    n = round(gx ** (1 / 3))
+    return (j % n * n + (j // n + j) % n) * n + (j // n**2 + j) % n
+
+
 def z_table(gy, forward):
     shape = (2 * KZ, NZ)
     row = lax.broadcasted_iota(jnp.int32, shape, 0)
     cell = lax.broadcasted_iota(jnp.int32, shape, 1)
     own = KZ // gy
-    mode = row // (2 * own) * own + row % own
+    mode = near_order(row // (2 * own), gy) * own + row % own
     imaginary = row // own % 2 == 1
     turn = jnp.where(imaginary, NZ // 4, 0)
     angle = ((mode * cell + turn) % NZ).astype(F32) * (2.0 * math.pi / NZ)
@@ -48,9 +57,10 @@
     return (jnp.cos(angle) * scale).astype(BF16)
 
 
-def y_waves(gy, xl, order):
+def y_waves(gx, gy, xl, order):
     both = np.stack(waves(kept_freqs(KY), np.arange(NY), NY))[order] / math.sqrt(NY)
     both = both.reshape(2, KY, gy, NY // gy)
+    both = both[:, far_order(np.arange(gx), gx)][:, :, near_order(np.arange(gy), gy)]
     table = np.einsum("tksy,ab->tsakby", both, np.eye(xl))
     return table.reshape(2, gy, xl * KY, xl * (NY // gy)).astype(jnp.bfloat16)
 
@@ -61,7 +71,7 @@
     pair = np.stack([np.stack([cosine, -sign * sine]), np.stack([sign * sine, cosine])])
     if not forward:
         pair = pair.swapaxes(0, 1)
-    pair = pair.reshape(2, 2, KX, gx, xl) / math.sqrt(NX)
+    pair = pair.reshape(2, 2, KX, gx, xl)[:, :, :, far_order(np.arange(gx), gx)] / math.sqrt(NX)
     return pair.transpose(4, 3, 0, 1, 2).reshape(xl, 2 * gx, 2 * KX).astype(jnp.bfloat16)
 
 
@@ -82,9 +92,13 @@
     return jnp.concatenate([ref[(*outer, last)], ref[(*outer, last + 1)]], axis=1)
 
 
-def rotated(gx, gy):
+def near_groups(gx, gy):
+    return [[a * gy + near_order(j, gy) for j in range(gy)] for a in range(gx)]
+
+
+def far_groups(gx, gy):
     step = gx // gy
-    return [[(j + step * g) % gx * gy + g for j in range(gx)] for g in range(gy)]
+    return [[far_order((j + step * g) % gx, gx) * gy + g for j in range(gx)] for g in range(gy)]
 
 
 def turn(cells, gx, gy, back):
@@ -94,7 +108,7 @@
     return pltpu.roll(cells, shift, 0)
 
 
-def z_forward_kernel(field_ref, _, out_ref, rows):
+def z_forward_kernel(field_ref, out_ref, rows):
     channels, xl, yl, nz = field_ref.shape
     table = z_table(out_ref.shape[0], True)
     for c in range(channels):
@@ -227,22 +241,21 @@
     mode_rows = jax.ShapeDtypeStruct((gx, 2, xl * columns), BF16)
     small = pltpu.CompilerParams(vmem_limit_bytes=16 * MIB)
 
-    def exchange(blocks):
-        groups = rotated(gx, gy)
+    def exchange(blocks, groups):
         return lax.all_to_all(blocks, ("gx", "gy"), 0, 0, axis_index_groups=groups, tiled=True)
 
     weight = spectral_weight[:, 0].transpose(1, 3, 4, 2, 0).reshape(columns, channels, 2 * KX)
     modes = pl.pallas_call(
         z_forward_kernel,
-        in_specs=[vmem(), pl.BlockSpec(memory_space=pl.ANY)],
+        in_specs=[vmem()],
         out_specs=vmem(),
         out_shape=pencil,
         scratch_shapes=[pltpu.VMEM((2 * KZ * channels, lanes), F32)],
         compiler_params=small,
         name="z_forward",
-    )(field, weight)
-
-    modes = lax.all_to_all(modes, "gy", 0, 0, tiled=True)
+    )(field)
+
+    modes = exchange(modes, near_groups(gx, gy))
     modes = pl.pallas_call(
         y_forward_kernel,
         in_specs=[vmem(), vmem()],
@@ -251,9 +264,9 @@
         scratch_shapes=[pltpu.VMEM((pl.cdiv(xl * columns, LANES), 2 * gx, LANES), F32)],
         compiler_params=small,
         name="y_forward",
-    )(modes, y_waves(gy, xl, [0, 1]))
-
-    modes = exchange(modes)
+    )(modes, y_waves(gx, gy, xl, [0, 1]))
+
+    modes = exchange(modes, far_groups(gx, gy))
 
     modes = pl.pallas_call(
         functools.partial(mix_kernel, gy),
@@ -264,7 +277,7 @@
         name="mix",
     )(modes, x_pair(gx, xl, True), weight, x_pair(gx, xl, False))
 
-    modes = exchange(modes)
+    modes = exchange(modes, far_groups(gx, gy))
 
     modes = pl.pallas_call(
         y_inverse_kernel,
@@ -274,9 +287,9 @@
         scratch_shapes=[pltpu.VMEM((pl.cdiv(xl * columns, LANES), 2 * gx, LANES), F32)],
         compiler_params=small,
         name="y_inverse",
-    )(modes, y_waves(gy, xl, [1, 0]))
-
-    modes = lax.all_to_all(modes, "gy", 0, 0, tiled=True)
+    )(modes, y_waves(gx, gy, xl, [1, 0]))
+
+    modes = exchange(modes, near_groups(gx, gy))
 
     return pl.pallas_call(
         output_kernel,

time: 99.1 us -> 98.8 us (level)
  blocking collectives: 88.3 us -> 64 us
  starting transfers between devices: 0 us -> 18.3 us
  waiting for transfers between devices: 0 us -> 3.97 us
  local copies, waits for them, and re-layouts: 4.04 us -> 5.18 us
    all_to_all x2 -> x0, blocking collectives: 41.8 us -> none  [per_device(): modes = lax.all_to_all(modes, 'gy', 0, 0, tiled=True)]
    all_to_all x0 -> x1, starting transfers between devices: none -> 18.3 us  [exchange(): lax.all_to_all(blocks, ('gx', 'gy'), 0, 0, axis_index_groups=groups, tile...]
    all_to_all x2 -> x3, blocking collectives: 46.5 us -> 64 us  [exchange(): lax.all_to_all(blocks, ('gx', 'gy'), 0, 0, axis_index_groups=groups, tile...]
    all_to_all x0 -> x1, waiting for transfers between devices: none -> 3.97 us  [exchange(): lax.all_to_all(blocks, ('gx', 'gy'), 0, 0, axis_index_groups=groups, tile...]
    unnamed x14, local copies, waits for them, and re-layouts: 1.76 us -> 2.98 us
  transfers between devices with their start and end apart: 0 -> 1, of which waited for: 0 -> 1; matrix products, arithmetic and copies ran while one was open for 0% -> 2% of each run, Pallas kernels for 0% -> 0%
where the time goes in v2:
time: 98.8 us; the launch traced here: 98.5 us
  blocking collectives  64 us (65%)
  starting transfers between devices  18.3 us (19%)
  Pallas kernels  6.99 us (7%)
  local copies, waits for them, and re-layouts  5.18 us (5%)
  waiting for transfers between devices  3.97 us (4%)
    all_to_all x3, blocking collectives, exchange(): lax.all_to_all(blocks, ('gx', 'gy'), 0, 0, axis_index_groups=groups, tile...  64 us
    all_to_all x1, starting transfers between devices, exchange(): lax.all_to_all(blocks, ('gx', 'gy'), 0, 0, axis_index_groups=groups, tile...  18.3 us
    all_to_all x1, waiting for transfers between devices, exchange(): lax.all_to_all(blocks, ('gx', 'gy'), 0, 0, axis_index_groups=groups, tile...  3.97 us
    pallas_call x1, Pallas kernels, per_device(): pl.pallas_call(output_kernel, in_specs=[vmem(), vmem(), vmem(), pl.BlockS...  3.19 us
    unnamed x14, local copies, waits for them, and re-layouts  2.98 us
    reshape x1, local copies, waits for them, and re-layouts, per_device(): spectral_weight[:, 0].transpose(1, 3, 4, 2, 0)  2.2 us
  transfers between devices with their start and end apart: 1, of which 1 were waited for; matrix products, arithmetic and copies ran while one was open for 2% of the time, Pallas kernels for 0%

profile of v2, /device:TPU:1, one launch (start us, length us, event | category | flops | bytes accessed | tf_op | source)
XLA Modules:
  0.0 98.5 jit_solution(1379658326720422745)
XLA Ops:
  0.0 0.0 copy-start
  0.0 1.7 %copy-done = f32[20,4,32,256]{3,2,1,0:T(8,128)S(1)} copy-done((f32[20,4,32,256]{3,2,1,0:T(8,128)S(1)}, f32[20,4,32,256]{3,2,1,0:T(8,128)}, u32[]{:S(2)}) %copy-start) | copy-done | bytes 2621464
  1.7 0.0 copy-start.3
  1.7 0.0 copy-start.4
  1.7 0.8 z_forward.1
  2.6 19.8 %all_to_all.20.modes_ref = bf16[8,160,128]{2,1,0:T(8,128)(2,1)S(1)} all-to-all(bf16[8,160,128]{2,1,0:T(8,128)(2,1)S(1)} %z_forward.1), channel_id=1, replica_groups={{0,6,1,7,2,4,3,5},{8,14,9,15,10,12,11,13},{16,22,17,23,18,20,19,21},{24..., dimensions={0} | all-to-all | bytes 655360 | tf_op jit(solution)/shard_map/all_to_all | solution.py:245
  22.4 0.0 copy-done.3
  22.4 1.4 %y_forward.1 = bf16[64,2,320]{2,1,0:T(2,128)(2,1)} custom-call(bf16[8,160,128]{2,1,0:T(8,128)(2,1)S(1)} %all_to_all.20.modes_ref, bf16[2,8,256,128]{3,2,1,0:T(8,128)(2,1)S(1)} %copy-done.3), custom_call_target="tpu_custom_call" | custom-call | tf_op jit(solution)/shard_map/y_forward/pallas_call | solution.py:259
  23.8 0.0 copy-start.1
  23.8 0.0 copy-start.5
  23.8 0.0 copy-start.6
  23.8 18.3 %all-to-all-start.1 = ((bf16[64,2,320]{2,1,0:T(2,128)(2,1)}), bf16[64,2,320]{2,1,0:T(2,128)(2,1)S(1)}, u32[]{:S(2)}, u32[]{:S(2)}) async-start(bf16[64,2,320]{2,1,0:T(2,128)(2,1)} %y_forward.1), calls=%async_computation.1 | async-start | bytes 196608 | tf_op jit(solution)/shard_map/all_to_all | solution.py:245
  42.1 2.2 %reshape.4.weight_ref = bf16[80,20,128]{2,1,0:T(8,128)(2,1)S(1)} reshape(bf16[4,20,20,2,64]{4,3,2,1,0:T(2,128)(2,1)} %bitcast.3) | data formatting | bytes 819200 | tf_op jit(solution)/shard_map/reshape | solution.py:247
  44.3 4.0 %all-to-all-done.1.modes_ref = bf16[64,2,320]{2,1,0:T(2,128)(2,1)S(1)} async-done(((bf16[64,2,320]{2,1,0:T(2,128)(2,1)}), bf16[64,2,320]{2,1,0:T(2,128)(2,1)S(1)}, u32[]{:S(2)}, u32[]{:S(2)}) %all-to-all-start.1) | async-done | bytes 81952 | tf_op jit(solution)/shard_map/all_to_all | solution.py:245
  48.3 0.0 copy-done.4
  48.3 1.0 %mix.1 = bf16[64,2,320]{2,1,0:T(2,128)(2,1)S(1)} custom-call(bf16[64,2,320]{2,1,0:T(2,128)(2,1)S(1)} %all-to-all-done.1.modes_ref, bf16[4,128,128]{2,1,0:T(8,128)(2,1)S(1)} %copy-done.4, bf16[80,20,128]{2,1,0:T(8,128)(2,1)S(1)} %reshape.4.weight_ref, bf16[4,128,128]{2,1,0:T(8,128)(2,1)S(1)} %copy-done.4), custom_call_target="tpu_custom_call" | custom-call | tf_op jit(solution)/shard_map/mix/pallas_call | solution.py:271
  49.4 21.7 %all_to_all.21.modes_ref = bf16[64,2,320]{2,1,0:T(2,128)(2,1)S(1)} all-to-all(bf16[64,2,320]{2,1,0:T(2,128)(2,1)S(1)} %mix.1), channel_id=1, replica_groups={{0,168,336,504,32,200,368,408,64,232,272,440,96,136,304,472,8,176,344,4..., dimensions={0} | all-to-all | bytes 163840 | tf_op jit(solution)/shard_map/all_to_all | solution.py:245
  71.1 0.0 copy-start.2
  71.1 1.2 %copy-done.2 = bf16[2,8,256,128]{3,2,1,0:T(8,128)(2,1)S(1)} copy-done((bf16[2,8,256,128]{3,2,1,0:T(8,128)(2,1)S(1)}, bf16[2,8,256,128]{3,2,1,0:T(8,128)(2,1)}, u32[]{:S(2)}) %copy-start.2) | copy-done | bytes 1048600
  72.3 0.5 y_inverse.1
  72.9 22.4 %all_to_all.22.modes_ref = bf16[8,160,128]{2,1,0:T(8,128)(2,1)S(1)} all-to-all(bf16[8,160,128]{2,1,0:T(8,128)(2,1)S(1)} %y_inverse.1), channel_id=1, replica_groups={{0,6,1,7,2,4,3,5},{8,14,9,15,10,12,11,13},{16,22,17,23,18,20,19,21},{24..., dimensions={0} | all-to-all | bytes 655360 | tf_op jit(solution)/shard_map/all_to_all | solution.py:245
  95.3 0.0 copy-done.1
  95.3 0.0 copy-done.5
  95.3 0.0 copy-done.6
  95.3 3.2 %output.1 = bf16[20,4,32,256]{3,2,1,0:T(8,128)(2,1)} custom-call(bf16[8,160,128]{2,1,0:T(8,128)(2,1)S(1)} %all_to_all.22.modes_ref, f32[20,4,32,256]{3,2,1,0:T(8,128)S(1)} %copy-done.1, f32[20,20]{1,0:T(8,128)S(1)} %copy-done.5, f32[20]{0:T(128)S(1)} %copy-done.6), custom_call_target="tpu_custom_call" | custom-call | tf_op jit(solution)/shard_map/output/pallas_call | solution.py:294
Async XLA Ops:
  0.0 1.7 %copy-start = (f32[20,4,32,256]{3,2,1,0:T(8,128)S(1)}, f32[20,4,32,256]{3,2,1,0:T(8,128)}, u32[]{:S(2)}) copy-start(f32[20,4,32,256]{3,2,1,0:T(8,128)} %field_ref.3) | copy-start | bytes 7864324
  1.7 20.7 %copy-start.3 = (bf16[2,8,256,128]{3,2,1,0:T(8,128)(2,1)S(1)}, bf16[2,8,256,128]{3,2,1,0:T(8,128)(2,1)}, u32[]{:S(2)}) copy-start(bf16[2,8,256,128]{3,2,1,0:T(8,128)(2,1)} %constant.6.clone.table_ref) | copy-start | bytes 3145732
  1.7 46.6 %copy-start.4 = (bf16[4,128,128]{2,1,0:T(8,128)(2,1)S(1)}, bf16[4,128,128]{2,1,0:T(8,128)(2,1)}, u32[]{:S(2)}) copy-start(bf16[4,128,128]{2,1,0:T(8,128)(2,1)} %constant.7.clone.forward_ref.inverse_ref) | copy-start | bytes 393220
  23.8 71.5 %copy-start.1 = (f32[20,4,32,256]{3,2,1,0:T(8,128)S(1)}, f32[20,4,32,256]{3,2,1,0:T(8,128)}, u32[]{:S(2)}) copy-start(f32[20,4,32,256]{3,2,1,0:T(8,128)} %field_ref.3) | copy-start | bytes 7864324
  23.8 71.5 %copy-start.5 = (f32[20,20]{1,0:T(8,128)S(1)}, f32[20,20]{1,0:T(8,128)}, u32[]{:S(2)}) copy-start(f32[20,20]{1,0:T(8,128)} %point_ref.1) | copy-start | bytes 4804
  23.8 71.5 %copy-start.6 = (f32[20]{0:T(128)S(1)}, f32[20]{0:T(128)}, u32[]{:S(2)}) copy-start(f32[20]{0:T(128)} %bias_ref.1) | copy-start | bytes 244
  23.8 24.5 %all-to-all-start.1 = ((bf16[64,2,320]{2,1,0:T(2,128)(2,1)}), bf16[64,2,320]{2,1,0:T(2,128)(2,1)S(1)}, u32[]{:S(2)}, u32[]{:S(2)}) async-start(bf16[64,2,320]{2,1,0:T(2,128)(2,1)} %y_forward.1), calls=%async_computation.1 | async-start | bytes 196608 | tf_op jit(solution)/shard_map/all_to_all | solution.py:245
  71.1 1.2 %copy-start.2 = (bf16[2,8,256,128]{3,2,1,0:T(8,128)(2,1)S(1)}, bf16[2,8,256,128]{3,2,1,0:T(8,128)(2,1)}, u32[]{:S(2)}) copy-start(bf16[2,8,256,128]{3,2,1,0:T(8,128)(2,1)} %constant.8.clone.table_ref) | copy-start | bytes 3145732

commit v3 on v2

--- a/solution.py
+++ b/solution.py
@@ -19,7 +19,6 @@
 F32 = jnp.float32
 BF16 = jnp.bfloat16
 MIB = 1 << 20
-CHUNK = 4
 LANES = 128
 
 
@@ -138,7 +137,7 @@
     out_ref[...] = joined[:, : out_ref.shape[2]].reshape(out_ref.shape).astype(BF16)
 
 
-def mix_kernel(gy, modes_ref, forward_ref, weight_ref, inverse_ref, out_ref):
+def mix_kernel(gy, modes_ref, forward_ref, weight_ref, inverse_ref, _, out_ref):
     xl = forward_ref.shape[0]
     columns = modes_ref.shape[2] // xl
     kz = columns // C
@@ -196,37 +195,54 @@
 
 
 def output_kernel(
-    modes_ref, field_ref, point_ref, bias_ref, out_ref, rows, point, result, sems
+    modes_ref, field_ref, point_ref, bias_ref, out_ref, rows, columns, result, sems
 ):
     channels, xl, yl, nz = field_ref.shape
     sub = 8
     size = channels * sub
+    depth = 2 * KZ
+    ones_at = depth + size
+    lane = lax.broadcasted_iota(jnp.int32, (channels, 2 * LANES), 1)
+    channel = lax.broadcasted_iota(jnp.int32, (channels, 2 * LANES), 0)
+    spot = jnp.where((lane - depth) // sub == channel, 1.0, 0.0)
+    spot = jnp.where((lane >= depth) & (lane < ones_at), spot, 0.0).astype(BF16)
+    weight = dot(point_ref[...].astype(BF16), spot, 0, 0)
+    bias = jnp.zeros((channels, 2 * LANES), F32)
+    for c in range(channels):
+        bias = jnp.where(channel == c, bias_ref[c], bias)
+    high = bias.astype(BF16).astype(F32)
+    weight = jnp.where(lane == ones_at, high, weight)
+    weight = jnp.where(lane == ones_at + 1, bias - high, weight).astype(BF16)
     row = lax.broadcasted_iota(jnp.int32, (size, channels), 0) // sub
     col = lax.broadcasted_iota(jnp.int32, (size, channels), 1)
     pick = jnp.where(row == col, 1.0, 0.0).astype(BF16)
-    tall = dot(pick, point_ref[...].astype(BF16), 1, 1).astype(BF16)
-    first = lax.broadcasted_iota(jnp.int32, (size, size), 0) % sub
-    second = lax.broadcasted_iota(jnp.int32, (size, size), 1) % sub
-    spread = jnp.where(first == second, dot(tall, pick, 1, 1), 0.0).astype(BF16)
+    first = lax.broadcasted_iota(jnp.int32, (size, 2 * LANES), 0) % sub
+    second = lax.broadcasted_iota(jnp.int32, (size, 2 * LANES), 1)
+    fixed = jnp.where((first == second % sub) | (second >= ones_at), dot(pick, weight, 1, 0), 0.0)
+    left, right = fixed[:, :LANES], fixed[:, LANES:].astype(BF16)
+
+    table = z_table(modes_ref.shape[0], False)
+    ones = jnp.ones((2 * LANES - ones_at, nz), BF16)
+    rows[...] = modes_ref[...].reshape(rows.shape).astype(F32)
+    blank = jnp.zeros((xl * yl, LANES - depth), F32)
+    for c in range(channels):
+        modes = rows[pl.ds(c, depth, stride=channels), :]
+        columns[c] = jnp.concatenate([modes.T, blank], axis=1)
+    copies = []
     for x in range(xl):
-        for y in range(0, yl, sub):
-            cells = field_ref[:, x, y : y + sub, :].reshape(size, nz).astype(BF16)
-            point[:, x, y : y + sub, :] = dot(spread, cells, 1, 0).reshape(channels, sub, nz)
-    rows[...] = modes_ref[...].reshape(rows.shape).astype(F32)
-    table = z_table(modes_ref.shape[0], False)
-    copies = []
-    for c in range(channels):
-        modes = rows[pl.ds(c, 2 * KZ, stride=channels), :].astype(BF16)
-        value = point[c].reshape(xl * yl, nz) + dot(modes, table, 0, 0) + bias_ref[c]
-        inner = value * (0.7978845608028654 + 0.035677408136300125 * value * value)
-        half = 0.5 * value
-        result[c] = (half + half * jnp.tanh(inner)).astype(BF16).reshape(xl, yl, nz)
-        if c % CHUNK == CHUNK - 1:
-            part = pl.ds(c + 1 - CHUNK, CHUNK)
-            copies.append(
-                pltpu.make_async_copy(result.at[part], out_ref.at[part], sems.at[c // CHUNK])
-            )
-            copies[-1].start()
+        for y in range(0, yl, 2 * sub):
+            halves = []
+            for h in (y, y + sub):
+                cells = field_ref[:, x, h : h + sub, :].reshape(size, nz).astype(BF16)
+                modes = columns[:, x * yl + h : x * yl + h + sub, :].reshape(size, LANES)
+                modes = jnp.concatenate([(modes + left).astype(BF16), right], axis=1)
+                value = dot(modes, jnp.concatenate([table, cells, ones], axis=0), 1, 0)
+                inner = value * (0.7978845608028654 + 0.035677408136300125 * value * value)
+                half = 0.5 * value
+                halves.append((half + half * jnp.tanh(inner)).reshape(channels, sub, nz))
+            result[:, x, y : y + 2 * sub, :] = jnp.concatenate(halves, axis=1).astype(BF16)
+        copies.append(pltpu.make_async_copy(result.at[:, x], out_ref.at[:, x], sems.at[x]))
+        copies[-1].start()
     for copy in copies:
         copy.wait()
 
@@ -268,14 +284,15 @@
 
     modes = exchange(modes, far_groups(gx, gy))
 
+    inverse = jnp.asarray(y_waves(gx, gy, xl, [1, 0]))
     modes = pl.pallas_call(
         functools.partial(mix_kernel, gy),
-        in_specs=[vmem(), vmem(), vmem(), vmem()],
+        in_specs=[vmem(), vmem(), vmem(), vmem(), pl.BlockSpec(memory_space=pl.ANY)],
         out_specs=vmem(),
         out_shape=mode_rows,
         compiler_params=small,
         name="mix",
-    )(modes, x_pair(gx, xl, True), weight, x_pair(gx, xl, False))
+    )(modes, x_pair(gx, xl, True), weight, x_pair(gx, xl, False), inverse)
 
     modes = exchange(modes, far_groups(gx, gy))
 
@@ -287,7 +304,7 @@
         scratch_shapes=[pltpu.VMEM((pl.cdiv(xl * columns, LANES), 2 * gx, LANES), F32)],
         compiler_params=small,
         name="y_inverse",
-    )(modes, y_waves(gx, gy, xl, [1, 0]))
+    )(modes, inverse)
 
     modes = exchange(modes, near_groups(gx, gy))
 
@@ -298,9 +315,9 @@
         out_shape=jax.ShapeDtypeStruct(field.shape, BF16),
         scratch_shapes=[
             pltpu.VMEM((2 * KZ * channels, lanes), F32),
-            pltpu.VMEM(field.shape, F32),
+            pltpu.VMEM((channels, lanes, LANES), F32),
             pltpu.VMEM(field.shape, BF16),
-            pltpu.SemaphoreType.DMA((channels // CHUNK,)),
+            pltpu.SemaphoreType.DMA((xl,)),
         ],
         compiler_params=small,
         name="output",

time: 98.8 us -> 99.5 us (level)
  local copies, waits for them, and re-layouts: 5.18 us -> 6.56 us
    unnamed x14 -> x16, local copies, waits for them, and re-layouts: 2.98 us -> 4.21 us
where the time goes in v3:
time: 99.5 us; the launch traced here: 99.1 us
  blocking collectives  64 us (64%)
  starting transfers between devices  18.1 us (18%)
  Pallas kernels  6.65 us (7%)
  local copies, waits for them, and re-layouts  6.56 us (7%)
  waiting for transfers between devices  3.8 us (4%)
    all_to_all x3, blocking collectives, exchange(): lax.all_to_all(blocks, ('gx', 'gy'), 0, 0, axis_index_groups=groups, tile...  64 us
    all_to_all x1, starting transfers between devices, exchange(): lax.all_to_all(blocks, ('gx', 'gy'), 0, 0, axis_index_groups=groups, tile...  18.1 us
    unnamed x16, local copies, waits for them, and re-layouts  4.21 us
    all_to_all x1, waiting for transfers between devices, exchange(): lax.all_to_all(blocks, ('gx', 'gy'), 0, 0, axis_index_groups=groups, tile...  3.8 us
    pallas_call x1, Pallas kernels, per_device(): pl.pallas_call(output_kernel, in_specs=[vmem(), vmem(), vmem(), pl.BlockS...  2.85 us
    reshape x1, local copies, waits for them, and re-layouts, per_device(): spectral_weight[:, 0].transpose(1, 3, 4, 2, 0)  2.35 us
  transfers between devices with their start and end apart: 1, of which 1 were waited for; matrix products, arithmetic and copies ran while one was open for 2% of the time, Pallas kernels for 0%

profile of v3, /device:TPU:1, one launch (start us, length us, event | category | flops | bytes accessed | tf_op | source)
XLA Modules:
  0.0 99.1 jit_solution(3693682738567014959)
XLA Ops:
  0.0 0.0 copy-start
  0.0 1.7 %copy-done = f32[20,4,32,256]{3,2,1,0:T(8,128)S(1)} copy-done((f32[20,4,32,256]{3,2,1,0:T(8,128)S(1)}, f32[20,4,32,256]{3,2,1,0:T(8,128)}, u32[]{:S(2)}) %copy-start) | copy-done | bytes 2621464
  1.7 0.0 copy-start.4
  1.7 0.0 copy-start.5
  1.7 0.8 z_forward.1
  2.6 19.8 %all_to_all.20.modes_ref = bf16[8,160,128]{2,1,0:T(8,128)(2,1)S(1)} all-to-all(bf16[8,160,128]{2,1,0:T(8,128)(2,1)S(1)} %z_forward.1), channel_id=1, replica_groups={{0,6,1,7,2,4,3,5},{8,14,9,15,10,12,11,13},{16,22,17,23,18,20,19,21},{24..., dimensions={0} | all-to-all | bytes 655360 | tf_op jit(solution)/shard_map/all_to_all | solution.py:261
  22.4 0.0 copy-done.4
  22.4 1.4 %y_forward.1 = bf16[64,2,320]{2,1,0:T(2,128)(2,1)} custom-call(bf16[8,160,128]{2,1,0:T(8,128)(2,1)S(1)} %all_to_all.20.modes_ref, bf16[2,8,256,128]{3,2,1,0:T(8,128)(2,1)S(1)} %copy-done.4), custom_call_target="tpu_custom_call" | custom-call | tf_op jit(solution)/shard_map/y_forward/pallas_call | solution.py:275
  23.8 18.1 %all-to-all-start.1 = ((bf16[64,2,320]{2,1,0:T(2,128)(2,1)}), bf16[64,2,320]{2,1,0:T(2,128)(2,1)S(1)}, u32[]{:S(2)}, u32[]{:S(2)}) async-start(bf16[64,2,320]{2,1,0:T(2,128)(2,1)} %y_forward.1), calls=%async_computation.1 | async-start | bytes 196608 | tf_op jit(solution)/shard_map/all_to_all | solution.py:261
  41.9 0.0 copy-start.7
  41.9 0.0 copy-start.1
  41.9 2.3 %reshape.4.weight_ref = bf16[80,20,128]{2,1,0:T(8,128)(2,1)S(1)} reshape(bf16[4,20,20,2,64]{4,3,2,1,0:T(2,128)(2,1)} %bitcast.3) | data formatting | bytes 819200 | tf_op jit(solution)/shard_map/reshape | solution.py:263
  44.3 3.8 %all-to-all-done.1.modes_ref = bf16[64,2,320]{2,1,0:T(2,128)(2,1)S(1)} async-done(((bf16[64,2,320]{2,1,0:T(2,128)(2,1)}), bf16[64,2,320]{2,1,0:T(2,128)(2,1)S(1)}, u32[]{:S(2)}, u32[]{:S(2)}) %all-to-all-start.1) | async-done | bytes 81952 | tf_op jit(solution)/shard_map/all_to_all | solution.py:261
  48.1 0.0 copy-done.5
  48.1 0.0 copy-start.2
  48.1 1.2 %copy-done.2 = bf16[2,8,256,128]{3,2,1,0:T(8,128)(2,1)S(1)} copy-done((bf16[2,8,256,128]{3,2,1,0:T(8,128)(2,1)S(1)}, bf16[2,8,256,128]{3,2,1,0:T(8,128)(2,1)}, u32[]{:S(2)}) %copy-start.2) | copy-done | bytes 1048600
  49.3 0.0 copy-start.6
  49.3 1.1 %mix.1 = bf16[64,2,320]{2,1,0:T(2,128)(2,1)S(1)} custom-call(bf16[64,2,320]{2,1,0:T(2,128)(2,1)S(1)} %all-to-all-done.1.modes_ref, bf16[4,128,128]{2,1,0:T(8,128)(2,1)S(1)} %copy-done.5, bf16[80,20,128]{2,1,0:T(8,128)(2,1)S(1)} %reshape.4.weight_ref, bf16[4,128,128]{2,1,0:T(8,128)(2,1)S(1)} %copy-done.5, bf16[2,8,256,128]{3,2,1,0:T(8,128)(2,1)S(1)} %copy-done.2), custom_call_target="tpu_custom_call" | custom-call | tf_op jit(solution)/shard_map/mix/pallas_call | solution.py:288
  50.3 21.7 %all_to_all.21.modes_ref = bf16[64,2,320]{2,1,0:T(2,128)(2,1)S(1)} all-to-all(bf16[64,2,320]{2,1,0:T(2,128)(2,1)S(1)} %mix.1), channel_id=1, replica_groups={{0,168,336,504,32,200,368,408,64,232,272,440,96,136,304,472,8,176,344,4..., dimensions={0} | all-to-all | bytes 163840 | tf_op jit(solution)/shard_map/all_to_all | solution.py:261
  72.1 0.0 copy-start.3
  72.1 1.2 %copy-done.3 = bf16[2,8,256,128]{3,2,1,0:T(8,128)(2,1)S(1)} copy-done((bf16[2,8,256,128]{3,2,1,0:T(8,128)(2,1)S(1)}, bf16[2,8,256,128]{3,2,1,0:T(8,128)(2,1)}, u32[]{:S(2)}) %copy-start.3) | copy-done | bytes 1048600
  73.3 0.5 y_inverse.1
  73.8 22.4 %all_to_all.22.modes_ref = bf16[8,160,128]{2,1,0:T(8,128)(2,1)S(1)} all-to-all(bf16[8,160,128]{2,1,0:T(8,128)(2,1)S(1)} %y_inverse.1), channel_id=1, replica_groups={{0,6,1,7,2,4,3,5},{8,14,9,15,10,12,11,13},{16,22,17,23,18,20,19,21},{24..., dimensions={0} | all-to-all | bytes 655360 | tf_op jit(solution)/shard_map/all_to_all | solution.py:261
  96.2 0.0 copy-done.7
  96.2 0.0 copy-done.1
  96.2 0.0 copy-done.6
  96.3 2.8 %output.1 = bf16[20,4,32,256]{3,2,1,0:T(8,128)(2,1)} custom-call(bf16[8,160,128]{2,1,0:T(8,128)(2,1)S(1)} %all_to_all.22.modes_ref, f32[20,4,32,256]{3,2,1,0:T(8,128)S(1)} %copy-done.1, f32[20,20]{1,0:T(8,128)S(1)} %copy-done.6, f32[20]{0:T(128)S(1)} %copy-done.7), custom_call_target="tpu_custom_call" | custom-call | tf_op jit(solution)/shard_map/output/pallas_call | solution.py:311
Async XLA Ops:
  0.0 1.7 %copy-start = (f32[20,4,32,256]{3,2,1,0:T(8,128)S(1)}, f32[20,4,32,256]{3,2,1,0:T(8,128)}, u32[]{:S(2)}) copy-start(f32[20,4,32,256]{3,2,1,0:T(8,128)} %field_ref.3) | copy-start | bytes 7864324
  1.7 20.7 %copy-start.4 = (bf16[2,8,256,128]{3,2,1,0:T(8,128)(2,1)S(1)}, bf16[2,8,256,128]{3,2,1,0:T(8,128)(2,1)}, u32[]{:S(2)}) copy-start(bf16[2,8,256,128]{3,2,1,0:T(8,128)(2,1)} %constant.6.clone.table_ref) | copy-start | bytes 3145732
  1.7 46.3 %copy-start.5 = (bf16[4,128,128]{2,1,0:T(8,128)(2,1)S(1)}, bf16[4,128,128]{2,1,0:T(8,128)(2,1)}, u32[]{:S(2)}) copy-start(bf16[4,128,128]{2,1,0:T(8,128)(2,1)} %constant.8.clone.forward_ref.inverse_ref) | copy-start | bytes 393220
  23.8 24.3 %all-to-all-start.1 = ((bf16[64,2,320]{2,1,0:T(2,128)(2,1)}), bf16[64,2,320]{2,1,0:T(2,128)(2,1)S(1)}, u32[]{:S(2)}, u32[]{:S(2)}) async-start(bf16[64,2,320]{2,1,0:T(2,128)(2,1)} %y_forward.1), calls=%async_computation.1 | async-start | bytes 196608 | tf_op jit(solution)/shard_map/all_to_all | solution.py:261
  41.9 54.4 %copy-start.7 = (f32[20]{0:T(128)S(1)}, f32[20]{0:T(128)}, u32[]{:S(2)}) copy-start(f32[20]{0:T(128)} %bias_ref.1) | copy-start | bytes 244
  41.9 54.4 %copy-start.1 = (f32[20,4,32,256]{3,2,1,0:T(8,128)S(1)}, f32[20,4,32,256]{3,2,1,0:T(8,128)}, u32[]{:S(2)}) copy-start(f32[20,4,32,256]{3,2,1,0:T(8,128)} %field_ref.3) | copy-start | bytes 7864324
  48.1 1.2 %copy-start.2 = (bf16[2,8,256,128]{3,2,1,0:T(8,128)(2,1)S(1)}, bf16[2,8,256,128]{3,2,1,0:T(8,128)(2,1)}, u32[]{:S(2)}) copy-start(bf16[2,8,256,128]{3,2,1,0:T(8,128)(2,1)} %constant.7.clone._.table_ref) | copy-start | bytes 3145732
  49.3 47.0 %copy-start.6 = (f32[20,20]{1,0:T(8,128)S(1)}, f32[20,20]{1,0:T(8,128)}, u32[]{:S(2)}) copy-start(f32[20,20]{1,0:T(8,128)} %point_ref.1) | copy-start | bytes 4804
  72.1 1.2 %copy-start.3 = (bf16[2,8,256,128]{3,2,1,0:T(8,128)(2,1)S(1)}, bf16[2,8,256,128]{3,2,1,0:T(8,128)(2,1)}, u32[]{:S(2)}) copy-start(bf16[2,8,256,128]{3,2,1,0:T(8,128)(2,1)} %constant.7.clone._.table_ref) | copy-start | bytes 3145732

commit v4 on v3

--- a/solution.py
+++ b/solution.py
@@ -20,6 +20,7 @@
 BF16 = jnp.bfloat16
 MIB = 1 << 20
 LANES = 128
+TURN = 3
 
 
 def kept_freqs(number):
@@ -96,27 +97,30 @@
 
 
 def far_groups(gx, gy):
-    step = gx // gy
-    return [[far_order((j + step * g) % gx, gx) * gy + g for j in range(gx)] for g in range(gy)]
+    turns = [gx // gy * (TURN * g + 1) % gx for g in range(gy)]
+    return [[far_order((j + turns[g]) % gx, gx) * gy + g for j in range(gx)] for g in range(gy)]
 
 
 def turn(cells, gx, gy, back):
-    shift = 2 * (gx // gy) * lax.axis_index("gy")
+    shift = 2 * lax.rem(gx // gy * (TURN * lax.axis_index("gy") + 1), gx)
     if not back:
         shift = lax.rem(2 * gx - shift, 2 * gx)
     return pltpu.roll(cells, shift, 0)
 
 
-def z_forward_kernel(field_ref, out_ref, rows):
+def z_forward_kernel(field_ref, weight_ref, out_ref, weight_out, rows, sem):
+    copy = pltpu.make_async_copy(weight_ref, weight_out, sem)
+    copy.start()
     channels, xl, yl, nz = field_ref.shape
     table = z_table(out_ref.shape[0], True)
     for c in range(channels):
         cells = field_ref[c].reshape(xl * yl, nz).astype(BF16)
         rows[pl.ds(c, 2 * KZ, stride=channels), :] = dot(table, cells, 1, 1)
     out_ref[...] = rows[...].astype(BF16).reshape(out_ref.shape)
-
-
-def y_forward_kernel(modes_ref, table_ref, out_ref, rows):
+    copy.wait()
+
+
+def y_forward_kernel(modes_ref, table_ref, _, out_ref, rows):
     gy, size, _ = modes_ref.shape
     columns = size // 2
     straight, crossed = 0.0, 0.0
@@ -137,7 +141,7 @@
     out_ref[...] = joined[:, : out_ref.shape[2]].reshape(out_ref.shape).astype(BF16)
 
 
-def mix_kernel(gy, modes_ref, forward_ref, weight_ref, inverse_ref, _, out_ref):
+def mix_kernel(gy, modes_ref, forward_ref, weight_ref, inverse_ref, out_ref):
     xl = forward_ref.shape[0]
     columns = modes_ref.shape[2] // xl
     kz = columns // C
@@ -260,39 +264,43 @@
     def exchange(blocks, groups):
         return lax.all_to_all(blocks, ("gx", "gy"), 0, 0, axis_index_groups=groups, tiled=True)
 
-    weight = spectral_weight[:, 0].transpose(1, 3, 4, 2, 0).reshape(columns, channels, 2 * KX)
-    modes = pl.pallas_call(
+    weight = spectral_weight[:, 0].transpose(1, 3, 4, 2, 0)
+    modes, weight = pl.pallas_call(
         z_forward_kernel,
-        in_specs=[vmem()],
-        out_specs=vmem(),
-        out_shape=pencil,
-        scratch_shapes=[pltpu.VMEM((2 * KZ * channels, lanes), F32)],
+        in_specs=[vmem(), hbm()],
+        out_specs=[vmem(), vmem()],
+        out_shape=[pencil, jax.ShapeDtypeStruct(weight.shape, BF16)],
+        scratch_shapes=[
+            pltpu.VMEM((2 * KZ * channels, lanes), F32),
+            pltpu.SemaphoreType.DMA,
+        ],
         compiler_params=small,
         name="z_forward",
-    )(field)
+    )(field, weight)
 
     modes = exchange(modes, near_groups(gx, gy))
+    modes, weight = lax.optimization_barrier((modes, weight))
+    weight = weight.reshape(columns, channels, 2 * KX)
     modes = pl.pallas_call(
         y_forward_kernel,
-        in_specs=[vmem(), vmem()],
+        in_specs=[vmem(), vmem(), pl.BlockSpec(memory_space=pl.ANY)],
         out_specs=vmem(),
         out_shape=mode_rows,
         scratch_shapes=[pltpu.VMEM((pl.cdiv(xl * columns, LANES), 2 * gx, LANES), F32)],
         compiler_params=small,
         name="y_forward",
-    )(modes, y_waves(gx, gy, xl, [0, 1]))
+    )(modes, y_waves(gx, gy, xl, [0, 1]), weight)
 
     modes = exchange(modes, far_groups(gx, gy))
 
-    inverse = jnp.asarray(y_waves(gx, gy, xl, [1, 0]))
     modes = pl.pallas_call(
         functools.partial(mix_kernel, gy),
-        in_specs=[vmem(), vmem(), vmem(), vmem(), pl.BlockSpec(memory_space=pl.ANY)],
+        in_specs=[vmem(), vmem(), vmem(), vmem()],
         out_specs=vmem(),
         out_shape=mode_rows,
         compiler_params=small,
         name="mix",
-    )(modes, x_pair(gx, xl, True), weight, x_pair(gx, xl, False), inverse)
+    )(modes, x_pair(gx, xl, True), weight, x_pair(gx, xl, False))
 
     modes = exchange(modes, far_groups(gx, gy))
 
@@ -304,7 +312,7 @@
         scratch_shapes=[pltpu.VMEM((pl.cdiv(xl * columns, LANES), 2 * gx, LANES), F32)],
         compiler_params=small,
         name="y_inverse",
-    )(modes, inverse)
+    )(modes, y_waves(gx, gy, xl, [1, 0]))
 
     modes = exchange(modes, near_groups(gx, gy))
 

time: 99.5 us -> 98.7 us (level)
  blocking collectives: 64 us -> 86.2 us
  starting transfers between devices: 18.1 us -> 0 us
  waiting for transfers between devices: 3.8 us -> 0 us
    all_to_all x3 -> x4, blocking collectives: 64 us -> 86.2 us  [exchange(): lax.all_to_all(blocks, ('gx', 'gy'), 0, 0, axis_index_groups=groups, tile...]
    all_to_all x1 -> x0, starting transfers between devices: 18.1 us -> none  [exchange(): lax.all_to_all(blocks, ('gx', 'gy'), 0, 0, axis_index_groups=groups, tile...]
    all_to_all x1 -> x0, waiting for transfers between devices: 3.8 us -> none  [exchange(): lax.all_to_all(blocks, ('gx', 'gy'), 0, 0, axis_index_groups=groups, tile...]
    unnamed x16 -> x18, local copies, waits for them, and re-layouts: 4.21 us -> 3.8 us
  transfers between devices with their start and end apart: 1 -> 0, of which waited for: 1 -> 0; matrix products, arithmetic and copies ran while one was open for 2% -> 0% of each run, Pallas kernels for 0% -> 0%
where the time goes in v4:
time: 98.7 us; the launch traced here: 98.4 us
  blocking collectives  86.2 us (87%)
  Pallas kernels  6.09 us (6%)
  local copies, waits for them, and re-layouts  5.99 us (6%)
    all_to_all x4, blocking collectives, exchange(): lax.all_to_all(blocks, ('gx', 'gy'), 0, 0, axis_index_groups=groups, tile...  86.2 us
    unnamed x18, local copies, waits for them, and re-layouts  3.8 us
    pallas_call x1, Pallas kernels, per_device(): pl.pallas_call(output_kernel, in_specs=[vmem(), vmem(), vmem(), pl.BlockS...  2.82 us
    reshape x1, local copies, waits for them, and re-layouts, per_device(): weight = weight.reshape(columns, channels, 2 * KX)  2.19 us

profile of v4, /device:TPU:1, one launch (start us, length us, event | category | flops | bytes accessed | tf_op | source)
XLA Modules:
  0.0 98.4 jit_solution(11003011540015519488)
XLA Ops:
  0.0 0.0 copy-start
  0.0 1.7 %copy-done = f32[20,4,32,256]{3,2,1,0:T(8,128)S(1)} copy-done((f32[20,4,32,256]{3,2,1,0:T(8,128)S(1)}, f32[20,4,32,256]{3,2,1,0:T(8,128)}, u32[]{:S(2)}) %copy-start) | copy-done | bytes 2621464
  1.7 0.0 copy-start.5
  1.7 1.1 %copy-done.5 = bf16[64,1,4,2,20,20]{0,3,5,4,2,1:T(2,128)(2,1)S(1)} copy-done((bf16[64,1,4,2,20,20]{0,3,5,4,2,1:T(2,128)(2,1)S(1)}, bf16[64,1,4,2,20,20]{0,3,5,4,2,1:T(2,128)(2,1)}, u32[]{:S(2)}) %copy-start.5) | copy-done | bytes 409624
  2.9 0.0 copy-start.3
  2.9 0.9 z_forward.1
  3.8 0.0 copy-start.4
  3.8 0.9 copy-done.4
  4.7 0.0 copy-start.6
  4.7 0.0 copy-start.2
  4.7 19.9 %all_to_all.20.modes_ref = bf16[8,160,128]{2,1,0:T(8,128)(2,1)S(1)} all-to-all(bf16[8,160,128]{2,1,0:T(8,128)(2,1)S(1)} %get-tuple-element.9), channel_id=1, replica_groups={{0,6,1,7,2,4,3,5},{8,14,9,15,10,12,11,13},{16,22,17,23,18,20,19,21},{24..., dimensions={0} | all-to-all | bytes 655360 | tf_op jit(solution)/shard_map/all_to_all | solution.py:265
  24.7 2.2 %reshape.4._.weight_ref = bf16[80,20,128]{2,1,0:T(8,128)(2,1)S(1)} reshape(bf16[4,20,20,2,64]{4,3,2,1,0:T(2,128)(2,1)} %copy-done.4) | data formatting | bytes 819200 | tf_op jit(solution)/shard_map/reshape | solution.py:283
  26.9 0.0 copy-done.3
  26.9 0.0 copy-start.1
  26.9 0.0 copy-start.7
  26.9 0.0 copy-start.8
  26.9 0.8 y_forward.1
  27.7 30.3 %all_to_all.21.modes_ref = bf16[64,2,320]{2,1,0:T(2,128)(2,1)S(1)} all-to-all(bf16[64,2,320]{2,1,0:T(2,128)(2,1)S(1)} %y_forward.1), channel_id=1, replica_groups={{64,232,272,440,96,136,304,472,8,176,344,480,40,208,376,384,72,240,280,..., dimensions={0} | all-to-all | bytes 163840 | tf_op jit(solution)/shard_map/all_to_all | solution.py:265
  57.9 0.0 copy-done.6
  57.9 1.0 %mix.1 = bf16[64,2,320]{2,1,0:T(2,128)(2,1)S(1)} custom-call(bf16[64,2,320]{2,1,0:T(2,128)(2,1)S(1)} %all_to_all.21.modes_ref, bf16[4,128,128]{2,1,0:T(8,128)(2,1)S(1)} %copy-done.6, bf16[80,20,128]{2,1,0:T(8,128)(2,1)S(1)} %reshape.4._.weight_ref, bf16[4,128,128]{2,1,0:T(8,128)(2,1)S(1)} %copy-done.6), custom_call_target="tpu_custom_call" | custom-call | tf_op jit(solution)/shard_map/mix/pallas_call | solution.py:296
  59.0 21.8 %all_to_all.22.modes_ref = bf16[64,2,320]{2,1,0:T(2,128)(2,1)S(1)} all-to-all(bf16[64,2,320]{2,1,0:T(2,128)(2,1)S(1)} %mix.1), channel_id=1, replica_groups={{64,232,272,440,96,136,304,472,8,176,344,480,40,208,376,384,72,240,280,..., dimensions={0} | all-to-all | bytes 163840 | tf_op jit(solution)/shard_map/all_to_all | solution.py:265
  80.8 0.0 copy-done.2
  80.8 0.5 y_inverse.1
  81.3 14.2 %all_to_all.23.modes_ref = bf16[8,160,128]{2,1,0:T(8,128)(2,1)S(1)} all-to-all(bf16[8,160,128]{2,1,0:T(8,128)(2,1)S(1)} %y_inverse.1), channel_id=1, replica_groups={{0,6,1,7,2,4,3,5},{8,14,9,15,10,12,11,13},{16,22,17,23,18,20,19,21},{24..., dimensions={0} | all-to-all | bytes 655360 | tf_op jit(solution)/shard_map/all_to_all | solution.py:265
  95.5 0.0 copy-done.1
  95.5 0.0 copy-done.7
  95.6 0.0 copy-done.8
  95.6 2.8 %output.1 = bf16[20,4,32,256]{3,2,1,0:T(8,128)(2,1)} custom-call(bf16[8,160,128]{2,1,0:T(8,128)(2,1)S(1)} %all_to_all.23.modes_ref, f32[20,4,32,256]{3,2,1,0:T(8,128)S(1)} %copy-done.1, f32[20,20]{1,0:T(8,128)S(1)} %copy-done.7, f32[20]{0:T(128)S(1)} %copy-done.8), custom_call_target="tpu_custom_call" | custom-call | tf_op jit(solution)/shard_map/output/pallas_call | solution.py:319
Async XLA Ops:
  0.0 1.7 %copy-start = (f32[20,4,32,256]{3,2,1,0:T(8,128)S(1)}, f32[20,4,32,256]{3,2,1,0:T(8,128)}, u32[]{:S(2)}) copy-start(f32[20,4,32,256]{3,2,1,0:T(8,128)} %field_ref.3) | copy-start | bytes 7864324
  1.7 1.1 %copy-start.5 = (bf16[64,1,4,2,20,20]{0,3,5,4,2,1:T(2,128)(2,1)S(1)}, bf16[64,1,4,2,20,20]{0,3,5,4,2,1:T(2,128)(2,1)}, u32[]{:S(2)}) copy-start(bf16[64,1,4,2,20,20]{0,3,5,4,2,1:T(2,128)(2,1)} %param.9) | copy-start | bytes 1228804
  2.9 24.0 %copy-start.3 = (bf16[2,8,256,128]{3,2,1,0:T(8,128)(2,1)S(1)}, bf16[2,8,256,128]{3,2,1,0:T(8,128)(2,1)}, u32[]{:S(2)}) copy-start(bf16[2,8,256,128]{3,2,1,0:T(8,128)(2,1)} %constant.6.clone.table_ref) | copy-start | bytes 3145732
  3.8 0.9 copy-start.4
  4.7 53.2 %copy-start.6 = (bf16[4,128,128]{2,1,0:T(8,128)(2,1)S(1)}, bf16[4,128,128]{2,1,0:T(8,128)(2,1)}, u32[]{:S(2)}) copy-start(bf16[4,128,128]{2,1,0:T(8,128)(2,1)} %constant.7.clone.forward_ref.inverse_ref) | copy-start | bytes 393220
  4.7 76.1 %copy-start.2 = (bf16[2,8,256,128]{3,2,1,0:T(8,128)(2,1)S(1)}, bf16[2,8,256,128]{3,2,1,0:T(8,128)(2,1)}, u32[]{:S(2)}) copy-start(bf16[2,8,256,128]{3,2,1,0:T(8,128)(2,1)} %constant.8.clone.table_ref) | copy-start | bytes 3145732
  26.9 68.7 %copy-start.1 = (f32[20,4,32,256]{3,2,1,0:T(8,128)S(1)}, f32[20,4,32,256]{3,2,1,0:T(8,128)}, u32[]{:S(2)}) copy-start(f32[20,4,32,256]{3,2,1,0:T(8,128)} %field_ref.3) | copy-start | bytes 7864324
  26.9 68.7 %copy-start.7 = (f32[20,20]{1,0:T(8,128)S(1)}, f32[20,20]{1,0:T(8,128)}, u32[]{:S(2)}) copy-start(f32[20,20]{1,0:T(8,128)} %point_ref.1) | copy-start | bytes 4804
  26.9 68.7 %copy-start.8 = (f32[20]{0:T(128)S(1)}, f32[20]{0:T(128)}, u32[]{:S(2)}) copy-start(f32[20]{0:T(128)} %bias_ref.1) | copy-start | bytes 244

commit v5 on v3

--- a/solution.py
+++ b/solution.py
@@ -20,6 +20,7 @@
 BF16 = jnp.bfloat16
 MIB = 1 << 20
 LANES = 128
+TURN = 3
 
 
 def kept_freqs(number):
@@ -96,12 +97,12 @@
 
 
 def far_groups(gx, gy):
-    step = gx // gy
-    return [[far_order((j + step * g) % gx, gx) * gy + g for j in range(gx)] for g in range(gy)]
+    turns = [gx // gy * (TURN * g + 1) % gx for g in range(gy)]
+    return [[far_order((j + turns[g]) % gx, gx) * gy + g for j in range(gx)] for g in range(gy)]
 
 
 def turn(cells, gx, gy, back):
-    shift = 2 * (gx // gy) * lax.axis_index("gy")
+    shift = 2 * lax.rem(gx // gy * (TURN * lax.axis_index("gy") + 1), gx)
     if not back:
         shift = lax.rem(2 * gx - shift, 2 * gx)
     return pltpu.roll(cells, shift, 0)
@@ -137,7 +138,7 @@
     out_ref[...] = joined[:, : out_ref.shape[2]].reshape(out_ref.shape).astype(BF16)
 
 
-def mix_kernel(gy, modes_ref, forward_ref, weight_ref, inverse_ref, _, out_ref):
+def mix_kernel(gy, modes_ref, forward_ref, weight_ref, inverse_ref, out_ref):
     xl = forward_ref.shape[0]
     columns = modes_ref.shape[2] // xl
     kz = columns // C
@@ -284,15 +285,14 @@
 
     modes = exchange(modes, far_groups(gx, gy))
 
-    inverse = jnp.asarray(y_waves(gx, gy, xl, [1, 0]))
     modes = pl.pallas_call(
         functools.partial(mix_kernel, gy),
-        in_specs=[vmem(), vmem(), vmem(), vmem(), pl.BlockSpec(memory_space=pl.ANY)],
+        in_specs=[vmem(), vmem(), vmem(), vmem()],
         out_specs=vmem(),
         out_shape=mode_rows,
         compiler_params=small,
         name="mix",
-    )(modes, x_pair(gx, xl, True), weight, x_pair(gx, xl, False), inverse)
+    )(modes, x_pair(gx, xl, True), weight, x_pair(gx, xl, False))
 
     modes = exchange(modes, far_groups(gx, gy))
 
@@ -304,7 +304,7 @@
         scratch_shapes=[pltpu.VMEM((pl.cdiv(xl * columns, LANES), 2 * gx, LANES), F32)],
         compiler_params=small,
         name="y_inverse",
-    )(modes, inverse)
+    )(modes, y_waves(gx, gy, xl, [1, 0]))
 
     modes = exchange(modes, near_groups(gx, gy))
 

time: 99.5 us -> 96.4 us (0.969)
  blocking collectives: 64 us -> 55.8 us
  waiting for transfers between devices: 3.8 us -> 11.4 us
  local copies, waits for them, and re-layouts: 6.56 us -> 5.18 us
  starting transfers between devices: 18.1 us -> 17 us
    all_to_all x3, blocking collectives: 64 us -> 55.8 us  [exchange(): lax.all_to_all(blocks, ('gx', 'gy'), 0, 0, axis_index_groups=groups, tile...]
    all_to_all x1, waiting for transfers between devices: 3.8 us -> 11.4 us  [exchange(): lax.all_to_all(blocks, ('gx', 'gy'), 0, 0, axis_index_groups=groups, tile...]
    unnamed x16 -> x14, local copies, waits for them, and re-layouts: 4.21 us -> 2.98 us
    all_to_all x1, starting transfers between devices: 18.1 us -> 17 us  [exchange(): lax.all_to_all(blocks, ('gx', 'gy'), 0, 0, axis_index_groups=groups, tile...]
where the time goes in v5:
time: 96.4 us; the launch traced here: 96 us
  blocking collectives  55.8 us (58%)
  starting transfers between devices  17 us (18%)
  waiting for transfers between devices  11.4 us (12%)
  Pallas kernels  6.61 us (7%)
  local copies, waits for them, and re-layouts  5.18 us (5%)
    all_to_all x3, blocking collectives, exchange(): lax.all_to_all(blocks, ('gx', 'gy'), 0, 0, axis_index_groups=groups, tile...  55.8 us
    all_to_all x1, starting transfers between devices, exchange(): lax.all_to_all(blocks, ('gx', 'gy'), 0, 0, axis_index_groups=groups, tile...  17 us
    all_to_all x1, waiting for transfers between devices, exchange(): lax.all_to_all(blocks, ('gx', 'gy'), 0, 0, axis_index_groups=groups, tile...  11.4 us
    unnamed x14, local copies, waits for them, and re-layouts  2.98 us
    pallas_call x1, Pallas kernels, per_device(): pl.pallas_call(output_kernel, in_specs=[vmem(), vmem(), vmem(), pl.BlockS...  2.82 us
    reshape x1, local copies, waits for them, and re-layouts, per_device(): spectral_weight[:, 0].transpose(1, 3, 4, 2, 0)  2.2 us
  transfers between devices with their start and end apart: 1, of which 1 were waited for; matrix products, arithmetic and copies ran while one was open for 2% of the time, Pallas kernels for 0%

profile of v5, /device:TPU:1, one launch (start us, length us, event | category | flops | bytes accessed | tf_op | source)
XLA Modules:
  0.0 96.0 jit_solution(3236171547232597666)
XLA Ops:
  0.0 0.0 copy-start
  0.0 1.7 %copy-done = f32[20,4,32,256]{3,2,1,0:T(8,128)S(1)} copy-done((f32[20,4,32,256]{3,2,1,0:T(8,128)S(1)}, f32[20,4,32,256]{3,2,1,0:T(8,128)}, u32[]{:S(2)}) %copy-start) | copy-done | bytes 2621464
  1.7 0.0 copy-start.3
  1.7 0.0 copy-start.4
  1.7 0.8 z_forward.1
  2.6 19.8 %all_to_all.20.modes_ref = bf16[8,160,128]{2,1,0:T(8,128)(2,1)S(1)} all-to-all(bf16[8,160,128]{2,1,0:T(8,128)(2,1)S(1)} %z_forward.1), channel_id=1, replica_groups={{0,6,1,7,2,4,3,5},{8,14,9,15,10,12,11,13},{16,22,17,23,18,20,19,21},{24..., dimensions={0} | all-to-all | bytes 655360 | tf_op jit(solution)/shard_map/all_to_all | solution.py:262
  22.4 0.0 copy-done.3
  22.4 1.4 %y_forward.1 = bf16[64,2,320]{2,1,0:T(2,128)(2,1)} custom-call(bf16[8,160,128]{2,1,0:T(8,128)(2,1)S(1)} %all_to_all.20.modes_ref, bf16[2,8,256,128]{3,2,1,0:T(8,128)(2,1)S(1)} %copy-done.3), custom_call_target="tpu_custom_call" | custom-call | tf_op jit(solution)/shard_map/y_forward/pallas_call | solution.py:276
  23.8 0.0 copy-start.1
  23.8 0.0 copy-start.5
  23.8 0.0 copy-start.6
  23.8 17.0 %all-to-all-start.1 = ((bf16[64,2,320]{2,1,0:T(2,128)(2,1)}), bf16[64,2,320]{2,1,0:T(2,128)(2,1)S(1)}, u32[]{:S(2)}, u32[]{:S(2)}) async-start(bf16[64,2,320]{2,1,0:T(2,128)(2,1)} %y_forward.1), calls=%async_computation.1 | async-start | bytes 196608 | tf_op jit(solution)/shard_map/all_to_all | solution.py:262
  40.8 2.2 %reshape.4.weight_ref = bf16[80,20,128]{2,1,0:T(8,128)(2,1)S(1)} reshape(bf16[4,20,20,2,64]{4,3,2,1,0:T(2,128)(2,1)} %bitcast.3) | data formatting | bytes 819200 | tf_op jit(solution)/shard_map/reshape | solution.py:264
  43.0 11.4 %all-to-all-done.1.modes_ref = bf16[64,2,320]{2,1,0:T(2,128)(2,1)S(1)} async-done(((bf16[64,2,320]{2,1,0:T(2,128)(2,1)}), bf16[64,2,320]{2,1,0:T(2,128)(2,1)S(1)}, u32[]{:S(2)}, u32[]{:S(2)}) %all-to-all-start.1) | async-done | bytes 81952 | tf_op jit(solution)/shard_map/all_to_all | solution.py:262
  54.4 0.0 copy-done.4
  54.4 1.0 %mix.1 = bf16[64,2,320]{2,1,0:T(2,128)(2,1)S(1)} custom-call(bf16[64,2,320]{2,1,0:T(2,128)(2,1)S(1)} %all-to-all-done.1.modes_ref, bf16[4,128,128]{2,1,0:T(8,128)(2,1)S(1)} %copy-done.4, bf16[80,20,128]{2,1,0:T(8,128)(2,1)S(1)} %reshape.4.weight_ref, bf16[4,128,128]{2,1,0:T(8,128)(2,1)S(1)} %copy-done.4), custom_call_target="tpu_custom_call" | custom-call | tf_op jit(solution)/shard_map/mix/pallas_call | solution.py:288
  55.5 21.4 %all_to_all.21.modes_ref = bf16[64,2,320]{2,1,0:T(2,128)(2,1)S(1)} all-to-all(bf16[64,2,320]{2,1,0:T(2,128)(2,1)S(1)} %mix.1), channel_id=1, replica_groups={{64,232,272,440,96,136,304,472,8,176,344,480,40,208,376,384,72,240,280,..., dimensions={0} | all-to-all | bytes 163840 | tf_op jit(solution)/shard_map/all_to_all | solution.py:262
  76.9 0.0 copy-start.2
  76.9 1.2 %copy-done.2 = bf16[2,8,256,128]{3,2,1,0:T(8,128)(2,1)S(1)} copy-done((bf16[2,8,256,128]{3,2,1,0:T(8,128)(2,1)S(1)}, bf16[2,8,256,128]{3,2,1,0:T(8,128)(2,1)}, u32[]{:S(2)}) %copy-start.2) | copy-done | bytes 1048600
  78.1 0.5 y_inverse.1
  78.7 14.5 %all_to_all.22.modes_ref = bf16[8,160,128]{2,1,0:T(8,128)(2,1)S(1)} all-to-all(bf16[8,160,128]{2,1,0:T(8,128)(2,1)S(1)} %y_inverse.1), channel_id=1, replica_groups={{0,6,1,7,2,4,3,5},{8,14,9,15,10,12,11,13},{16,22,17,23,18,20,19,21},{24..., dimensions={0} | all-to-all | bytes 655360 | tf_op jit(solution)/shard_map/all_to_all | solution.py:262
  93.2 0.0 copy-done.1
  93.2 0.0 copy-done.5
  93.2 0.0 copy-done.6
  93.2 2.8 %output.1 = bf16[20,4,32,256]{3,2,1,0:T(8,128)(2,1)} custom-call(bf16[8,160,128]{2,1,0:T(8,128)(2,1)S(1)} %all_to_all.22.modes_ref, f32[20,4,32,256]{3,2,1,0:T(8,128)S(1)} %copy-done.1, f32[20,20]{1,0:T(8,128)S(1)} %copy-done.5, f32[20]{0:T(128)S(1)} %copy-done.6), custom_call_target="tpu_custom_call" | custom-call | tf_op jit(solution)/shard_map/output/pallas_call | solution.py:311
Async XLA Ops:
  0.0 1.7 %copy-start = (f32[20,4,32,256]{3,2,1,0:T(8,128)S(1)}, f32[20,4,32,256]{3,2,1,0:T(8,128)}, u32[]{:S(2)}) copy-start(f32[20,4,32,256]{3,2,1,0:T(8,128)} %field_ref.3) | copy-start | bytes 7864324
  1.7 20.7 %copy-start.3 = (bf16[2,8,256,128]{3,2,1,0:T(8,128)(2,1)S(1)}, bf16[2,8,256,128]{3,2,1,0:T(8,128)(2,1)}, u32[]{:S(2)}) copy-start(bf16[2,8,256,128]{3,2,1,0:T(8,128)(2,1)} %constant.6.clone.table_ref) | copy-start | bytes 3145732
  1.7 52.7 %copy-start.4 = (bf16[4,128,128]{2,1,0:T(8,128)(2,1)S(1)}, bf16[4,128,128]{2,1,0:T(8,128)(2,1)}, u32[]{:S(2)}) copy-start(bf16[4,128,128]{2,1,0:T(8,128)(2,1)} %constant.7.clone.forward_ref.inverse_ref) | copy-start | bytes 393220
  23.8 69.4 %copy-start.1 = (f32[20,4,32,256]{3,2,1,0:T(8,128)S(1)}, f32[20,4,32,256]{3,2,1,0:T(8,128)}, u32[]{:S(2)}) copy-start(f32[20,4,32,256]{3,2,1,0:T(8,128)} %field_ref.3) | copy-start | bytes 7864324
  23.8 69.4 %copy-start.5 = (f32[20,20]{1,0:T(8,128)S(1)}, f32[20,20]{1,0:T(8,128)}, u32[]{:S(2)}) copy-start(f32[20,20]{1,0:T(8,128)} %point_ref.1) | copy-start | bytes 4804
  23.8 69.4 %copy-start.6 = (f32[20]{0:T(128)S(1)}, f32[20]{0:T(128)}, u32[]{:S(2)}) copy-start(f32[20]{0:T(128)} %bias_ref.1) | copy-start | bytes 244
  23.8 30.6 %all-to-all-start.1 = ((bf16[64,2,320]{2,1,0:T(2,128)(2,1)}), bf16[64,2,320]{2,1,0:T(2,128)(2,1)S(1)}, u32[]{:S(2)}, u32[]{:S(2)}) async-start(bf16[64,2,320]{2,1,0:T(2,128)(2,1)} %y_forward.1), calls=%async_computation.1 | async-start | bytes 196608 | tf_op jit(solution)/shard_map/all_to_all | solution.py:262
  76.9 1.2 %copy-start.2 = (bf16[2,8,256,128]{3,2,1,0:T(8,128)(2,1)S(1)}, bf16[2,8,256,128]{3,2,1,0:T(8,128)(2,1)}, u32[]{:S(2)}) copy-start(bf16[2,8,256,128]{3,2,1,0:T(8,128)(2,1)} %constant.8.clone.table_ref) | copy-start | bytes 3145732

commit v6 on v5

--- a/solution.py
+++ b/solution.py
@@ -97,12 +97,13 @@
 
 
 def far_groups(gx, gy):
-    turns = [gx // gy * (TURN * g + 1) % gx for g in range(gy)]
+    turns = [(gx // gy + 1) * ((TURN * g + 1) % gy) % gx for g in range(gy)]
     return [[far_order((j + turns[g]) % gx, gx) * gy + g for j in range(gx)] for g in range(gy)]
 
 
 def turn(cells, gx, gy, back):
-    shift = 2 * lax.rem(gx // gy * (TURN * lax.axis_index("gy") + 1), gx)
+    place = lax.rem(TURN * lax.axis_index("gy") + 1, gy)
+    shift = 2 * lax.rem((gx // gy + 1) * place, gx)
     if not back:
         shift = lax.rem(2 * gx - shift, 2 * gx)
     return pltpu.roll(cells, shift, 0)

time: 96.4 us -> 97.3 us (level)
  waiting for transfers between devices: 11.4 us -> 8.5 us
  blocking collectives: 55.8 us -> 57.8 us
  starting transfers between devices: 17 us -> 18.8 us
    all_to_all x1, waiting for transfers between devices: 11.4 us -> 8.5 us  [exchange(): lax.all_to_all(blocks, ('gx', 'gy'), 0, 0, axis_index_groups=groups, tile...]
    all_to_all x3, blocking collectives: 55.8 us -> 57.8 us  [exchange(): lax.all_to_all(blocks, ('gx', 'gy'), 0, 0, axis_index_groups=groups, tile...]
    all_to_all x1, starting transfers between devices: 17 us -> 18.8 us  [exchange(): lax.all_to_all(blocks, ('gx', 'gy'), 0, 0, axis_index_groups=groups, tile...]
where the time goes in v6:
time: 97.3 us; the launch traced here: 96.9 us
  blocking collectives  57.8 us (59%)
  starting transfers between devices  18.8 us (19%)
  waiting for transfers between devices  8.5 us (9%)
  Pallas kernels  6.62 us (7%)
  local copies, waits for them, and re-layouts  5.18 us (5%)
    all_to_all x3, blocking collectives, exchange(): lax.all_to_all(blocks, ('gx', 'gy'), 0, 0, axis_index_groups=groups, tile...  57.8 us
    all_to_all x1, starting transfers between devices, exchange(): lax.all_to_all(blocks, ('gx', 'gy'), 0, 0, axis_index_groups=groups, tile...  18.8 us
    all_to_all x1, waiting for transfers between devices, exchange(): lax.all_to_all(blocks, ('gx', 'gy'), 0, 0, axis_index_groups=groups, tile...  8.5 us
    unnamed x14, local copies, waits for them, and re-layouts  2.98 us
    pallas_call x1, Pallas kernels, per_device(): pl.pallas_call(output_kernel, in_specs=[vmem(), vmem(), vmem(), pl.BlockS...  2.82 us
    reshape x1, local copies, waits for them, and re-layouts, per_device(): spectral_weight[:, 0].transpose(1, 3, 4, 2, 0)  2.2 us
  transfers between devices with their start and end apart: 1, of which 1 were waited for; matrix products, arithmetic and copies ran while one was open for 2% of the time, Pallas kernels for 0%

profile of v6, /device:TPU:1, one launch (start us, length us, event | category | flops | bytes accessed | tf_op | source)
XLA Modules:
  0.0 96.9 jit_solution(14364596369323205447)
XLA Ops:
  0.0 0.0 copy-start
  0.0 1.7 %copy-done = f32[20,4,32,256]{3,2,1,0:T(8,128)S(1)} copy-done((f32[20,4,32,256]{3,2,1,0:T(8,128)S(1)}, f32[20,4,32,256]{3,2,1,0:T(8,128)}, u32[]{:S(2)}) %copy-start) | copy-done | bytes 2621464
  1.7 0.0 copy-start.3
  1.7 0.0 copy-start.4
  1.7 0.8 z_forward.1
  2.6 19.8 %all_to_all.20.modes_ref = bf16[8,160,128]{2,1,0:T(8,128)(2,1)S(1)} all-to-all(bf16[8,160,128]{2,1,0:T(8,128)(2,1)S(1)} %z_forward.1), channel_id=1, replica_groups={{0,6,1,7,2,4,3,5},{8,14,9,15,10,12,11,13},{16,22,17,23,18,20,19,21},{24..., dimensions={0} | all-to-all | bytes 655360 | tf_op jit(solution)/shard_map/all_to_all | solution.py:263
  22.4 0.0 copy-done.3
  22.4 1.4 %y_forward.1 = bf16[64,2,320]{2,1,0:T(2,128)(2,1)} custom-call(bf16[8,160,128]{2,1,0:T(8,128)(2,1)S(1)} %all_to_all.20.modes_ref, bf16[2,8,256,128]{3,2,1,0:T(8,128)(2,1)S(1)} %copy-done.3), custom_call_target="tpu_custom_call" | custom-call | tf_op jit(solution)/shard_map/y_forward/pallas_call | solution.py:277
  23.8 0.0 copy-start.1
  23.8 0.0 copy-start.5
  23.8 0.0 copy-start.6
  23.8 18.8 %all-to-all-start.1 = ((bf16[64,2,320]{2,1,0:T(2,128)(2,1)}), bf16[64,2,320]{2,1,0:T(2,128)(2,1)S(1)}, u32[]{:S(2)}, u32[]{:S(2)}) async-start(bf16[64,2,320]{2,1,0:T(2,128)(2,1)} %y_forward.1), calls=%async_computation.1 | async-start | bytes 196608 | tf_op jit(solution)/shard_map/all_to_all | solution.py:263
  42.6 2.2 %reshape.4.weight_ref = bf16[80,20,128]{2,1,0:T(8,128)(2,1)S(1)} reshape(bf16[4,20,20,2,64]{4,3,2,1,0:T(2,128)(2,1)} %bitcast.3) | data formatting | bytes 819200 | tf_op jit(solution)/shard_map/reshape | solution.py:265
  44.8 8.5 %all-to-all-done.1.modes_ref = bf16[64,2,320]{2,1,0:T(2,128)(2,1)S(1)} async-done(((bf16[64,2,320]{2,1,0:T(2,128)(2,1)}), bf16[64,2,320]{2,1,0:T(2,128)(2,1)S(1)}, u32[]{:S(2)}, u32[]{:S(2)}) %all-to-all-start.1) | async-done | bytes 81952 | tf_op jit(solution)/shard_map/all_to_all | solution.py:263
  53.3 0.0 copy-done.4
  53.3 1.1 %mix.1 = bf16[64,2,320]{2,1,0:T(2,128)(2,1)S(1)} custom-call(bf16[64,2,320]{2,1,0:T(2,128)(2,1)S(1)} %all-to-all-done.1.modes_ref, bf16[4,128,128]{2,1,0:T(8,128)(2,1)S(1)} %copy-done.4, bf16[80,20,128]{2,1,0:T(8,128)(2,1)S(1)} %reshape.4.weight_ref, bf16[4,128,128]{2,1,0:T(8,128)(2,1)S(1)} %copy-done.4), custom_call_target="tpu_custom_call" | custom-call | tf_op jit(solution)/shard_map/mix/pallas_call | solution.py:289
  54.4 22.0 %all_to_all.21.modes_ref = bf16[64,2,320]{2,1,0:T(2,128)(2,1)S(1)} all-to-all(bf16[64,2,320]{2,1,0:T(2,128)(2,1)S(1)} %mix.1), channel_id=1, replica_groups={{232,272,440,96,136,304,472,8,176,344,480,40,208,376,384,72,240,280,416..., dimensions={0} | all-to-all | bytes 163840 | tf_op jit(solution)/shard_map/all_to_all | solution.py:263
  76.4 0.0 copy-start.2
  76.4 1.2 %copy-done.2 = bf16[2,8,256,128]{3,2,1,0:T(8,128)(2,1)S(1)} copy-done((bf16[2,8,256,128]{3,2,1,0:T(8,128)(2,1)S(1)}, bf16[2,8,256,128]{3,2,1,0:T(8,128)(2,1)}, u32[]{:S(2)}) %copy-start.2) | copy-done | bytes 1048600
  77.6 0.5 y_inverse.1
  78.2 15.9 %all_to_all.22.modes_ref = bf16[8,160,128]{2,1,0:T(8,128)(2,1)S(1)} all-to-all(bf16[8,160,128]{2,1,0:T(8,128)(2,1)S(1)} %y_inverse.1), channel_id=1, replica_groups={{0,6,1,7,2,4,3,5},{8,14,9,15,10,12,11,13},{16,22,17,23,18,20,19,21},{24..., dimensions={0} | all-to-all | bytes 655360 | tf_op jit(solution)/shard_map/all_to_all | solution.py:263
  94.1 0.0 copy-done.1
  94.1 0.0 copy-done.5
  94.1 0.0 copy-done.6
  94.1 2.8 %output.1 = bf16[20,4,32,256]{3,2,1,0:T(8,128)(2,1)} custom-call(bf16[8,160,128]{2,1,0:T(8,128)(2,1)S(1)} %all_to_all.22.modes_ref, f32[20,4,32,256]{3,2,1,0:T(8,128)S(1)} %copy-done.1, f32[20,20]{1,0:T(8,128)S(1)} %copy-done.5, f32[20]{0:T(128)S(1)} %copy-done.6), custom_call_target="tpu_custom_call" | custom-call | tf_op jit(solution)/shard_map/output/pallas_call | solution.py:312
Async XLA Ops:
  0.0 1.7 %copy-start = (f32[20,4,32,256]{3,2,1,0:T(8,128)S(1)}, f32[20,4,32,256]{3,2,1,0:T(8,128)}, u32[]{:S(2)}) copy-start(f32[20,4,32,256]{3,2,1,0:T(8,128)} %field_ref.3) | copy-start | bytes 7864324
  1.7 20.7 %copy-start.3 = (bf16[2,8,256,128]{3,2,1,0:T(8,128)(2,1)S(1)}, bf16[2,8,256,128]{3,2,1,0:T(8,128)(2,1)}, u32[]{:S(2)}) copy-start(bf16[2,8,256,128]{3,2,1,0:T(8,128)(2,1)} %constant.6.clone.table_ref) | copy-start | bytes 3145732
  1.7 51.6 %copy-start.4 = (bf16[4,128,128]{2,1,0:T(8,128)(2,1)S(1)}, bf16[4,128,128]{2,1,0:T(8,128)(2,1)}, u32[]{:S(2)}) copy-start(bf16[4,128,128]{2,1,0:T(8,128)(2,1)} %constant.7.clone.forward_ref.inverse_ref) | copy-start | bytes 393220
  23.8 70.3 %copy-start.1 = (f32[20,4,32,256]{3,2,1,0:T(8,128)S(1)}, f32[20,4,32,256]{3,2,1,0:T(8,128)}, u32[]{:S(2)}) copy-start(f32[20,4,32,256]{3,2,1,0:T(8,128)} %field_ref.3) | copy-start | bytes 7864324
  23.8 70.3 %copy-start.5 = (f32[20,20]{1,0:T(8,128)S(1)}, f32[20,20]{1,0:T(8,128)}, u32[]{:S(2)}) copy-start(f32[20,20]{1,0:T(8,128)} %point_ref.1) | copy-start | bytes 4804
  23.8 70.3 %copy-start.6 = (f32[20]{0:T(128)S(1)}, f32[20]{0:T(128)}, u32[]{:S(2)}) copy-start(f32[20]{0:T(128)} %bias_ref.1) | copy-start | bytes 244
  23.8 29.5 %all-to-all-start.1 = ((bf16[64,2,320]{2,1,0:T(2,128)(2,1)}), bf16[64,2,320]{2,1,0:T(2,128)(2,1)S(1)}, u32[]{:S(2)}, u32[]{:S(2)}) async-start(bf16[64,2,320]{2,1,0:T(2,128)(2,1)} %y_forward.1), calls=%async_computation.1 | async-start | bytes 196608 | tf_op jit(solution)/shard_map/all_to_all | solution.py:263
  76.4 1.2 %copy-start.2 = (bf16[2,8,256,128]{3,2,1,0:T(8,128)(2,1)S(1)}, bf16[2,8,256,128]{3,2,1,0:T(8,128)(2,1)}, u32[]{:S(2)}) copy-start(bf16[2,8,256,128]{3,2,1,0:T(8,128)(2,1)} %constant.8.clone.table_ref) | copy-start | bytes 3145732

commit v7 on v5

--- a/solution.py
+++ b/solution.py
@@ -20,7 +20,6 @@
 BF16 = jnp.bfloat16
 MIB = 1 << 20
 LANES = 128
-TURN = 3
 
 
 def kept_freqs(number):
@@ -96,13 +95,17 @@
     return [[a * gy + near_order(j, gy) for j in range(gy)] for a in range(gx)]
 
 
+def turns_of(g):
+    return g // 2 * 16 + 8 - g % 2 * 6
+
+
 def far_groups(gx, gy):
-    turns = [gx // gy * (TURN * g + 1) % gx for g in range(gy)]
+    turns = [turns_of(g) % gx for g in range(gy)]
     return [[far_order((j + turns[g]) % gx, gx) * gy + g for j in range(gx)] for g in range(gy)]
 
 
 def turn(cells, gx, gy, back):
-    shift = 2 * lax.rem(gx // gy * (TURN * lax.axis_index("gy") + 1), gx)
+    shift = 2 * lax.rem(turns_of(lax.axis_index("gy")), gx)
     if not back:
         shift = lax.rem(2 * gx - shift, 2 * gx)
     return pltpu.roll(cells, shift, 0)

time: 96.4 us -> 93.7 us (0.972)
  waiting for transfers between devices: 11.4 us -> 1.7 us
  blocking collectives: 55.8 us -> 60.1 us
  starting transfers between devices: 17 us -> 19.7 us
    all_to_all x1, waiting for transfers between devices: 11.4 us -> 1.7 us  [exchange(): lax.all_to_all(blocks, ('gx', 'gy'), 0, 0, axis_index_groups=groups, tile...]
    all_to_all x3, blocking collectives: 55.8 us -> 60.1 us  [exchange(): lax.all_to_all(blocks, ('gx', 'gy'), 0, 0, axis_index_groups=groups, tile...]
    all_to_all x1, starting transfers between devices: 17 us -> 19.7 us  [exchange(): lax.all_to_all(blocks, ('gx', 'gy'), 0, 0, axis_index_groups=groups, tile...]
where the time goes in v7:
time: 93.7 us; the launch traced here: 93.4 us
  blocking collectives  60.1 us (64%)
  starting transfers between devices  19.7 us (21%)
  Pallas kernels  6.62 us (7%)
  local copies, waits for them, and re-layouts  5.18 us (6%)
  waiting for transfers between devices  1.7 us (2%)
    all_to_all x3, blocking collectives, exchange(): lax.all_to_all(blocks, ('gx', 'gy'), 0, 0, axis_index_groups=groups, tile...  60.1 us
    all_to_all x1, starting transfers between devices, exchange(): lax.all_to_all(blocks, ('gx', 'gy'), 0, 0, axis_index_groups=groups, tile...  19.7 us
    unnamed x14, local copies, waits for them, and re-layouts  2.98 us
    pallas_call x1, Pallas kernels, per_device(): pl.pallas_call(output_kernel, in_specs=[vmem(), vmem(), vmem(), pl.BlockS...  2.82 us
    reshape x1, local copies, waits for them, and re-layouts, per_device(): spectral_weight[:, 0].transpose(1, 3, 4, 2, 0)  2.2 us
  transfers between devices with their start and end apart: 1, of which 1 were waited for; matrix products, arithmetic and copies ran while one was open for 2% of the time, Pallas kernels for 0%

profile of v7, /device:TPU:1, one launch (start us, length us, event | category | flops | bytes accessed | tf_op | source)
XLA Modules:
  0.0 93.4 jit_solution(16485357141854971581)
XLA Ops:
  0.0 0.0 copy-start
  0.0 1.7 %copy-done = f32[20,4,32,256]{3,2,1,0:T(8,128)S(1)} copy-done((f32[20,4,32,256]{3,2,1,0:T(8,128)S(1)}, f32[20,4,32,256]{3,2,1,0:T(8,128)}, u32[]{:S(2)}) %copy-start) | copy-done | bytes 2621464
  1.7 0.0 copy-start.3
  1.7 0.0 copy-start.4
  1.7 0.8 z_forward.1
  2.6 19.8 %all_to_all.20.modes_ref = bf16[8,160,128]{2,1,0:T(8,128)(2,1)S(1)} all-to-all(bf16[8,160,128]{2,1,0:T(8,128)(2,1)S(1)} %z_forward.1), channel_id=1, replica_groups={{0,6,1,7,2,4,3,5},{8,14,9,15,10,12,11,13},{16,22,17,23,18,20,19,21},{24..., dimensions={0} | all-to-all | bytes 655360 | tf_op jit(solution)/shard_map/all_to_all | solution.py:265
  22.4 0.0 copy-done.3
  22.4 1.4 %y_forward.1 = bf16[64,2,320]{2,1,0:T(2,128)(2,1)} custom-call(bf16[8,160,128]{2,1,0:T(8,128)(2,1)S(1)} %all_to_all.20.modes_ref, bf16[2,8,256,128]{3,2,1,0:T(8,128)(2,1)S(1)} %copy-done.3), custom_call_target="tpu_custom_call" | custom-call | tf_op jit(solution)/shard_map/y_forward/pallas_call | solution.py:279
  23.8 0.0 copy-start.1
  23.8 0.0 copy-start.5
  23.8 0.0 copy-start.6
  23.8 19.7 %all-to-all-start.1 = ((bf16[64,2,320]{2,1,0:T(2,128)(2,1)}), bf16[64,2,320]{2,1,0:T(2,128)(2,1)S(1)}, u32[]{:S(2)}, u32[]{:S(2)}) async-start(bf16[64,2,320]{2,1,0:T(2,128)(2,1)} %y_forward.1), calls=%async_computation.1 | async-start | bytes 196608 | tf_op jit(solution)/shard_map/all_to_all | solution.py:265
  43.5 2.2 %reshape.4.weight_ref = bf16[80,20,128]{2,1,0:T(8,128)(2,1)S(1)} reshape(bf16[4,20,20,2,64]{4,3,2,1,0:T(2,128)(2,1)} %bitcast.3) | data formatting | bytes 819200 | tf_op jit(solution)/shard_map/reshape | solution.py:267
  45.8 1.7 %all-to-all-done.1.modes_ref = bf16[64,2,320]{2,1,0:T(2,128)(2,1)S(1)} async-done(((bf16[64,2,320]{2,1,0:T(2,128)(2,1)}), bf16[64,2,320]{2,1,0:T(2,128)(2,1)S(1)}, u32[]{:S(2)}, u32[]{:S(2)}) %all-to-all-start.1) | async-done | bytes 81952 | tf_op jit(solution)/shard_map/all_to_all | solution.py:265
  47.5 0.0 copy-done.4
  47.5 1.1 %mix.1 = bf16[64,2,320]{2,1,0:T(2,128)(2,1)S(1)} custom-call(bf16[64,2,320]{2,1,0:T(2,128)(2,1)S(1)} %all-to-all-done.1.modes_ref, bf16[4,128,128]{2,1,0:T(8,128)(2,1)S(1)} %copy-done.4, bf16[80,20,128]{2,1,0:T(8,128)(2,1)S(1)} %reshape.4.weight_ref, bf16[4,128,128]{2,1,0:T(8,128)(2,1)S(1)} %copy-done.4), custom_call_target="tpu_custom_call" | custom-call | tf_op jit(solution)/shard_map/mix/pallas_call | solution.py:291
  48.5 21.9 %all_to_all.21.modes_ref = bf16[64,2,320]{2,1,0:T(2,128)(2,1)S(1)} all-to-all(bf16[64,2,320]{2,1,0:T(2,128)(2,1)S(1)} %mix.1), channel_id=1, replica_groups={{64,232,272,440,96,136,304,472,8,176,344,480,40,208,376,384,72,240,280,..., dimensions={0} | all-to-all | bytes 163840 | tf_op jit(solution)/shard_map/all_to_all | solution.py:265
  70.4 0.0 copy-start.2
  70.4 1.2 %copy-done.2 = bf16[2,8,256,128]{3,2,1,0:T(8,128)(2,1)S(1)} copy-done((bf16[2,8,256,128]{3,2,1,0:T(8,128)(2,1)S(1)}, bf16[2,8,256,128]{3,2,1,0:T(8,128)(2,1)}, u32[]{:S(2)}) %copy-start.2) | copy-done | bytes 1048600
  71.6 0.5 y_inverse.1
  72.2 18.3 %all_to_all.22.modes_ref = bf16[8,160,128]{2,1,0:T(8,128)(2,1)S(1)} all-to-all(bf16[8,160,128]{2,1,0:T(8,128)(2,1)S(1)} %y_inverse.1), channel_id=1, replica_groups={{0,6,1,7,2,4,3,5},{8,14,9,15,10,12,11,13},{16,22,17,23,18,20,19,21},{24..., dimensions={0} | all-to-all | bytes 655360 | tf_op jit(solution)/shard_map/all_to_all | solution.py:265
  90.5 0.0 copy-done.1
  90.5 0.0 copy-done.5
  90.5 0.0 copy-done.6
  90.5 2.8 %output.1 = bf16[20,4,32,256]{3,2,1,0:T(8,128)(2,1)} custom-call(bf16[8,160,128]{2,1,0:T(8,128)(2,1)S(1)} %all_to_all.22.modes_ref, f32[20,4,32,256]{3,2,1,0:T(8,128)S(1)} %copy-done.1, f32[20,20]{1,0:T(8,128)S(1)} %copy-done.5, f32[20]{0:T(128)S(1)} %copy-done.6), custom_call_target="tpu_custom_call" | custom-call | tf_op jit(solution)/shard_map/output/pallas_call | solution.py:314
Async XLA Ops:
  0.0 1.7 %copy-start = (f32[20,4,32,256]{3,2,1,0:T(8,128)S(1)}, f32[20,4,32,256]{3,2,1,0:T(8,128)}, u32[]{:S(2)}) copy-start(f32[20,4,32,256]{3,2,1,0:T(8,128)} %field_ref.3) | copy-start | bytes 7864324
  1.7 20.7 %copy-start.3 = (bf16[2,8,256,128]{3,2,1,0:T(8,128)(2,1)S(1)}, bf16[2,8,256,128]{3,2,1,0:T(8,128)(2,1)}, u32[]{:S(2)}) copy-start(bf16[2,8,256,128]{3,2,1,0:T(8,128)(2,1)} %constant.6.clone.table_ref) | copy-start | bytes 3145732
  1.7 45.7 %copy-start.4 = (bf16[4,128,128]{2,1,0:T(8,128)(2,1)S(1)}, bf16[4,128,128]{2,1,0:T(8,128)(2,1)}, u32[]{:S(2)}) copy-start(bf16[4,128,128]{2,1,0:T(8,128)(2,1)} %constant.7.clone.forward_ref.inverse_ref) | copy-start | bytes 393220
  23.8 66.7 %copy-start.1 = (f32[20,4,32,256]{3,2,1,0:T(8,128)S(1)}, f32[20,4,32,256]{3,2,1,0:T(8,128)}, u32[]{:S(2)}) copy-start(f32[20,4,32,256]{3,2,1,0:T(8,128)} %field_ref.3) | copy-start | bytes 7864324
  23.8 66.7 %copy-start.5 = (f32[20,20]{1,0:T(8,128)S(1)}, f32[20,20]{1,0:T(8,128)}, u32[]{:S(2)}) copy-start(f32[20,20]{1,0:T(8,128)} %point_ref.1) | copy-start | bytes 4804
  23.8 66.7 %copy-start.6 = (f32[20]{0:T(128)S(1)}, f32[20]{0:T(128)}, u32[]{:S(2)}) copy-start(f32[20]{0:T(128)} %bias_ref.1) | copy-start | bytes 244
  23.8 23.7 %all-to-all-start.1 = ((bf16[64,2,320]{2,1,0:T(2,128)(2,1)}), bf16[64,2,320]{2,1,0:T(2,128)(2,1)S(1)}, u32[]{:S(2)}, u32[]{:S(2)}) async-start(bf16[64,2,320]{2,1,0:T(2,128)(2,1)} %y_forward.1), calls=%async_computation.1 | async-start | bytes 196608 | tf_op jit(solution)/shard_map/all_to_all | solution.py:265
  70.4 1.2 %copy-start.2 = (bf16[2,8,256,128]{3,2,1,0:T(8,128)(2,1)S(1)}, bf16[2,8,256,128]{3,2,1,0:T(8,128)(2,1)}, u32[]{:S(2)}) copy-start(bf16[2,8,256,128]{3,2,1,0:T(8,128)(2,1)} %constant.8.clone.table_ref) | copy-start | bytes 3145732

commit v8 on v7

--- a/solution.py
+++ b/solution.py
@@ -96,7 +96,8 @@
 
 
 def turns_of(g):
-    return g // 2 * 16 + 8 - g % 2 * 6
+    core = g % 2
+    return g // 2 * 16 + 8 - core * 6 + g // 2 % 2 * (core * 16 - 3)
 
 
 def far_groups(gx, gy):

time: 93.7 us -> 92.2 us (0.984)
  waiting for transfers between devices: 1.7 us -> 0.68 us
    all_to_all x1, waiting for transfers between devices: 1.7 us -> 0.68 us  [exchange(): lax.all_to_all(blocks, ('gx', 'gy'), 0, 0, axis_index_groups=groups, tile...]
where the time goes in v8:
time: 92.2 us; the launch traced here: 91.8 us
  blocking collectives  59.5 us (65%)
  starting transfers between devices  19.7 us (21%)
  Pallas kernels  6.63 us (7%)
  local copies, waits for them, and re-layouts  5.18 us (6%)
    all_to_all x3, blocking collectives, exchange(): lax.all_to_all(blocks, ('gx', 'gy'), 0, 0, axis_index_groups=groups, tile...  59.5 us
    all_to_all x1, starting transfers between devices, exchange(): lax.all_to_all(blocks, ('gx', 'gy'), 0, 0, axis_index_groups=groups, tile...  19.7 us
    unnamed x14, local copies, waits for them, and re-layouts  2.98 us
    pallas_call x1, Pallas kernels, per_device(): pl.pallas_call(output_kernel, in_specs=[vmem(), vmem(), vmem(), pl.BlockS...  2.82 us
    reshape x1, local copies, waits for them, and re-layouts, per_device(): spectral_weight[:, 0].transpose(1, 3, 4, 2, 0)  2.2 us
  transfers between devices with their start and end apart: 1, of which 1 were waited for; matrix products, arithmetic and copies ran while one was open for 2% of the time, Pallas kernels for 0%

profile of v8, /device:TPU:1, one launch (start us, length us, event | category | flops | bytes accessed | tf_op | source)
XLA Modules:
  0.0 91.8 jit_solution(8521742955627224119)
XLA Ops:
  0.0 0.0 copy-start
  0.0 1.7 %copy-done = f32[20,4,32,256]{3,2,1,0:T(8,128)S(1)} copy-done((f32[20,4,32,256]{3,2,1,0:T(8,128)S(1)}, f32[20,4,32,256]{3,2,1,0:T(8,128)}, u32[]{:S(2)}) %copy-start) | copy-done | bytes 2621464
  1.7 0.0 copy-start.3
  1.7 0.0 copy-start.4
  1.7 0.8 z_forward.1
  2.6 19.8 %all_to_all.20.modes_ref = bf16[8,160,128]{2,1,0:T(8,128)(2,1)S(1)} all-to-all(bf16[8,160,128]{2,1,0:T(8,128)(2,1)S(1)} %z_forward.1), channel_id=1, replica_groups={{0,6,1,7,2,4,3,5},{8,14,9,15,10,12,11,13},{16,22,17,23,18,20,19,21},{24..., dimensions={0} | all-to-all | bytes 655360 | tf_op jit(solution)/shard_map/all_to_all | solution.py:266
  22.4 0.0 copy-done.3
  22.4 1.4 %y_forward.1 = bf16[64,2,320]{2,1,0:T(2,128)(2,1)} custom-call(bf16[8,160,128]{2,1,0:T(8,128)(2,1)S(1)} %all_to_all.20.modes_ref, bf16[2,8,256,128]{3,2,1,0:T(8,128)(2,1)S(1)} %copy-done.3), custom_call_target="tpu_custom_call" | custom-call | tf_op jit(solution)/shard_map/y_forward/pallas_call | solution.py:280
  23.8 0.0 copy-start.1
  23.8 0.0 copy-start.5
  23.8 0.0 copy-start.6
  23.8 19.7 %all-to-all-start.1 = ((bf16[64,2,320]{2,1,0:T(2,128)(2,1)}), bf16[64,2,320]{2,1,0:T(2,128)(2,1)S(1)}, u32[]{:S(2)}, u32[]{:S(2)}) async-start(bf16[64,2,320]{2,1,0:T(2,128)(2,1)} %y_forward.1), calls=%async_computation.1 | async-start | bytes 196608 | tf_op jit(solution)/shard_map/all_to_all | solution.py:266
  43.5 2.2 %reshape.4.weight_ref = bf16[80,20,128]{2,1,0:T(8,128)(2,1)S(1)} reshape(bf16[4,20,20,2,64]{4,3,2,1,0:T(2,128)(2,1)} %bitcast.3) | data formatting | bytes 819200 | tf_op jit(solution)/shard_map/reshape | solution.py:268
  45.8 0.7 all-to-all-done.1.modes_ref
  46.4 0.0 copy-done.4
  46.4 1.1 %mix.1 = bf16[64,2,320]{2,1,0:T(2,128)(2,1)S(1)} custom-call(bf16[64,2,320]{2,1,0:T(2,128)(2,1)S(1)} %all-to-all-done.1.modes_ref, bf16[4,128,128]{2,1,0:T(8,128)(2,1)S(1)} %copy-done.4, bf16[80,20,128]{2,1,0:T(8,128)(2,1)S(1)} %reshape.4.weight_ref, bf16[4,128,128]{2,1,0:T(8,128)(2,1)S(1)} %copy-done.4), custom_call_target="tpu_custom_call" | custom-call | tf_op jit(solution)/shard_map/mix/pallas_call | solution.py:292
  47.5 22.3 %all_to_all.21.modes_ref = bf16[64,2,320]{2,1,0:T(2,128)(2,1)S(1)} all-to-all(bf16[64,2,320]{2,1,0:T(2,128)(2,1)S(1)} %mix.1), channel_id=1, replica_groups={{64,232,272,440,96,136,304,472,8,176,344,480,40,208,376,384,72,240,280,..., dimensions={0} | all-to-all | bytes 163840 | tf_op jit(solution)/shard_map/all_to_all | solution.py:266
  69.8 0.0 copy-start.2
  69.8 1.2 %copy-done.2 = bf16[2,8,256,128]{3,2,1,0:T(8,128)(2,1)S(1)} copy-done((bf16[2,8,256,128]{3,2,1,0:T(8,128)(2,1)S(1)}, bf16[2,8,256,128]{3,2,1,0:T(8,128)(2,1)}, u32[]{:S(2)}) %copy-start.2) | copy-done | bytes 1048600
  71.1 0.5 y_inverse.1
  71.6 17.4 %all_to_all.22.modes_ref = bf16[8,160,128]{2,1,0:T(8,128)(2,1)S(1)} all-to-all(bf16[8,160,128]{2,1,0:T(8,128)(2,1)S(1)} %y_inverse.1), channel_id=1, replica_groups={{0,6,1,7,2,4,3,5},{8,14,9,15,10,12,11,13},{16,22,17,23,18,20,19,21},{24..., dimensions={0} | all-to-all | bytes 655360 | tf_op jit(solution)/shard_map/all_to_all | solution.py:266
  89.0 0.0 copy-done.1
  89.0 0.0 copy-done.5
  89.0 0.0 copy-done.6
  89.0 2.8 %output.1 = bf16[20,4,32,256]{3,2,1,0:T(8,128)(2,1)} custom-call(bf16[8,160,128]{2,1,0:T(8,128)(2,1)S(1)} %all_to_all.22.modes_ref, f32[20,4,32,256]{3,2,1,0:T(8,128)S(1)} %copy-done.1, f32[20,20]{1,0:T(8,128)S(1)} %copy-done.5, f32[20]{0:T(128)S(1)} %copy-done.6), custom_call_target="tpu_custom_call" | custom-call | tf_op jit(solution)/shard_map/output/pallas_call | solution.py:315
Async XLA Ops:
  0.0 1.7 %copy-start = (f32[20,4,32,256]{3,2,1,0:T(8,128)S(1)}, f32[20,4,32,256]{3,2,1,0:T(8,128)}, u32[]{:S(2)}) copy-start(f32[20,4,32,256]{3,2,1,0:T(8,128)} %field_ref.3) | copy-start | bytes 7864324
  1.7 20.7 %copy-start.3 = (bf16[2,8,256,128]{3,2,1,0:T(8,128)(2,1)S(1)}, bf16[2,8,256,128]{3,2,1,0:T(8,128)(2,1)}, u32[]{:S(2)}) copy-start(bf16[2,8,256,128]{3,2,1,0:T(8,128)(2,1)} %constant.6.clone.table_ref) | copy-start | bytes 3145732
  1.7 44.7 %copy-start.4 = (bf16[4,128,128]{2,1,0:T(8,128)(2,1)S(1)}, bf16[4,128,128]{2,1,0:T(8,128)(2,1)}, u32[]{:S(2)}) copy-start(bf16[4,128,128]{2,1,0:T(8,128)(2,1)} %constant.7.clone.forward_ref.inverse_ref) | copy-start | bytes 393220
  23.8 65.2 %copy-start.1 = (f32[20,4,32,256]{3,2,1,0:T(8,128)S(1)}, f32[20,4,32,256]{3,2,1,0:T(8,128)}, u32[]{:S(2)}) copy-start(f32[20,4,32,256]{3,2,1,0:T(8,128)} %field_ref.3) | copy-start | bytes 7864324
  23.8 65.2 %copy-start.5 = (f32[20,20]{1,0:T(8,128)S(1)}, f32[20,20]{1,0:T(8,128)}, u32[]{:S(2)}) copy-start(f32[20,20]{1,0:T(8,128)} %point_ref.1) | copy-start | bytes 4804
  23.8 65.2 %copy-start.6 = (f32[20]{0:T(128)S(1)}, f32[20]{0:T(128)}, u32[]{:S(2)}) copy-start(f32[20]{0:T(128)} %bias_ref.1) | copy-start | bytes 244
  23.8 22.6 %all-to-all-start.1 = ((bf16[64,2,320]{2,1,0:T(2,128)(2,1)}), bf16[64,2,320]{2,1,0:T(2,128)(2,1)S(1)}, u32[]{:S(2)}, u32[]{:S(2)}) async-start(bf16[64,2,320]{2,1,0:T(2,128)(2,1)} %y_forward.1), calls=%async_computation.1 | async-start | bytes 196608 | tf_op jit(solution)/shard_map/all_to_all | solution.py:266
  69.8 1.2 %copy-start.2 = (bf16[2,8,256,128]{3,2,1,0:T(8,128)(2,1)S(1)}, bf16[2,8,256,128]{3,2,1,0:T(8,128)(2,1)}, u32[]{:S(2)}) copy-start(bf16[2,8,256,128]{3,2,1,0:T(8,128)(2,1)} %constant.8.clone.table_ref) | copy-start | bytes 3145732
